TPU v7x, 512 devices: a whole 4x8x8 slice. The times are simulated.
512 devices in a mesh: dp: 128 (over y, z, core), rep: 4 (over x).
Axes of the slice: x: 4, y: 8, z: 8, core: 2. Of those that a mesh axis runs over, the one named last changes fastest.
Arguments:
- tokens: bfloat16 [262144, 512], P(('dp', 'rep')), may hold values from -6 to 6
- owner_cotangent: bfloat16 [393216, 512], P(('dp', 'rep')), may hold values from -6 to 6
- proj_weight: bfloat16 [512, 2048], replicated, may hold values from -0.25 to 0.25
- out_weight: bfloat16 [512, 512], replicated, may hold values from -0.25 to 0.25
- bias_table: float32 [4, 10], replicated, may hold values from -1 to 1
- history_length: int32 [2048], P(('dp', 'rep')), may hold values from 1 to 512, as said below
- first_block: int32 [2048], P(('dp', 'rep')), may hold values from 0 to 3, as said below
- owner_slot: int32 [2048], P(('dp', 'rep')), may hold values from 0 to 3071, as said below
Outputs:
- token_grad: bfloat16 [262144, 512], P(('dp', 'rep'))
- proj_grad: float32 [512, 2048], P(None, ('dp', 'rep'))
- out_grad: float32 [512, 512], replicated
- bias_grad: float32 [4, 10], replicated
Inputs may be any that keep to these rules, and one draw needn't show every extreme that they name: `history_length`: A history of n blocks occupies n consecutive blocks of one aligned group of 4 blocks and has between (n - 1) * 128 + 1 and n * 128 tokens; all its blocks carry its length. `first_block`: all blocks of a history carry the offset, within their group of 4, of the history's first block. owner_slot = o * 6 + s. The owner o of a block on device (dp index d, rep index e) is the device (d + r mod 128, e), 0 <= r < 2, the same r for all blocks of a history; histories of more than 2 blocks have r = 0. Slots 0 to 3 of an owner take blocks of its own device; slots 4 + (r - 1) * 2 onward take at most 2 blocks of the device r steps back along dp. A history's blocks take consecutive slots in order; no slot takes two blocks. In every draw some device sends 2 blocks at a nonzero offset.
All inputs are finite; a program needn't handle non-finite values.
Results may differ from a plain program's by a relative error of at most 0.011.
Values may be sent and summed in bfloat16 or wider, within the bound.
A program may use at most 128 MiB of HBM per device.

v0:
```python
import jax
import jax.numpy as jnp
import numpy as np
from jax import lax
from jax.sharding import PartitionSpec as P

HEADS = 4
HEAD_DIM = 128
BLOCK = 128
REACH = 2
CAP = 2
BUCKETS = 10


EPSILON = 1e-06


def passed_along(value, axis, steps):
    count = lax.axis_size(axis)
    pairs = [(source, (source + steps) % count) for source in range(count)]
    return lax.ppermute(value, axis, pairs)


def norm_rows(values_in):
    centered = values_in - jnp.mean(values_in, axis=-1, keepdims=True)
    inverse = lax.rsqrt(jnp.mean(centered * centered, axis=-1, keepdims=True) + EPSILON)
    return (centered * inverse, inverse)


def norm_back(normed, inverse, upstream):
    return inverse * (
        upstream
        - jnp.mean(upstream, axis=-1, keepdims=True)
        - normed * jnp.mean(upstream * normed, axis=-1, keepdims=True)
    )


def buckets_of(distance):
    bucket = jnp.zeros(distance.shape, jnp.int32)
    for level_index in range(BUCKETS - 1):
        bucket = bucket + (distance >= 2**level_index).astype(jnp.int32)
    return bucket


def pair_logits(query_rows, key_rows, bias_table, query_pos, key_pos, seq_length):
    row_count = query_rows.shape[0]
    query_heads = query_rows.reshape(row_count, HEADS, HEAD_DIM)
    key_heads = key_rows.reshape(row_count, HEADS, HEAD_DIM)
    scores = jnp.einsum(
        "qhd,khd->hqk", query_heads, key_heads, preferred_element_type=jnp.float32
    ) * HEAD_DIM ** (-0.5)
    distance = query_pos[:, None] - key_pos[None, :]
    onehot = (buckets_of(distance)[:, :, None] == jnp.arange(BUCKETS, dtype=jnp.int32)).astype(
        jnp.float32
    )
    bias = jnp.einsum("qkb,hb->hqk", onehot, bias_table, precision=lax.Precision.HIGHEST)
    keep_mask = (
        (distance >= 0) & (key_pos[None, :] < seq_length) & (query_pos[:, None] < seq_length)
    ).astype(jnp.float32)
    return (scores + bias, keep_mask, onehot, query_heads, key_heads)


def pair_forward(query_rows, key_rows, value_rows, bias_table, query_pos, key_pos, seq_length):
    row_count = query_rows.shape[0]
    logits, keep_mask, onehot, query_heads, key_heads = pair_logits(
        query_rows, key_rows, bias_table, query_pos, key_pos, seq_length
    )
    weights = (jax.nn.silu(logits) * keep_mask).astype(jnp.bfloat16)
    value_heads = value_rows.reshape(row_count, HEADS, HEAD_DIM)
    mixed_heads = jnp.einsum(
        "hqk,khd->qhd", weights, value_heads, preferred_element_type=jnp.float32
    )
    return mixed_heads.reshape(row_count, HEADS * HEAD_DIM)


def pair_backward(
    query_rows, key_rows, value_rows, upstream, bias_table, query_pos, key_pos, seq_length
):
    row_count = query_rows.shape[0]
    logits, keep_mask, onehot, query_heads, key_heads = pair_logits(
        query_rows, key_rows, bias_table, query_pos, key_pos, seq_length
    )
    sigma = jax.nn.sigmoid(logits)
    weights = (jax.nn.silu(logits) * keep_mask).astype(jnp.bfloat16)
    value_heads = value_rows.reshape(row_count, HEADS, HEAD_DIM)
    upstream_heads = upstream.reshape(row_count, HEADS, HEAD_DIM)
    d_weights = jnp.einsum(
        "qhd,khd->hqk", upstream_heads, value_heads, preferred_element_type=jnp.float32
    )
    d_logits = d_weights * keep_mask * sigma * (1.0 + logits * (1.0 - sigma))
    d_table = jnp.einsum("hqk,qkb->hb", d_logits, onehot, precision=lax.Precision.HIGHEST)
    d_logits_b = d_logits.astype(jnp.bfloat16)
    d_query = jnp.einsum(
        "hqk,khd->qhd", d_logits_b, key_heads, preferred_element_type=jnp.float32
    ) * HEAD_DIM ** (-0.5)
    d_key = jnp.einsum(
        "hqk,qhd->khd", d_logits_b, query_heads, preferred_element_type=jnp.float32
    ) * HEAD_DIM ** (-0.5)
    d_value = jnp.einsum(
        "hqk,qhd->khd", weights, upstream_heads, preferred_element_type=jnp.float32
    )
    width_all = HEADS * HEAD_DIM
    return (
        d_query.reshape(row_count, width_all),
        d_key.reshape(row_count, width_all),
        d_value.reshape(row_count, width_all),
        d_table,
    )


def pick(stacked, where_at):
    return lax.dynamic_index_in_dim(stacked, where_at, 0, keepdims=False)


def add_at(stacked, where_at, addend):
    return lax.dynamic_update_index_in_dim(stacked, pick(stacked, where_at) + addend, where_at, 0)


def layer_grads(block_rows, cot_blocks, lengths, positions, proj_weight, out_weight, bias_table):
    block_count, row_count, model_width = block_rows.shape
    flat_rows = block_count * row_count
    inputs = block_rows.reshape(flat_rows, model_width).astype(jnp.float32)
    token_pos = positions[:, None] * row_count + jnp.arange(row_count, dtype=jnp.int32)[None, :]
    valid = (token_pos < lengths[:, None]).reshape(flat_rows, 1)
    normed, inverse = norm_rows(inputs)
    normed_b = normed.astype(jnp.bfloat16)
    proj = jnp.dot(normed_b, proj_weight, preferred_element_type=jnp.float32)
    sigma = jax.nn.sigmoid(proj)
    acts = jax.nn.silu(proj).astype(jnp.bfloat16)
    gate_part = acts[:, :model_width]
    value_part = acts[:, model_width : 2 * model_width].reshape(block_count, row_count, model_width)
    query_part = acts[:, 2 * model_width : 3 * model_width].reshape(
        block_count, row_count, model_width
    )
    key_part = acts[:, 3 * model_width :].reshape(block_count, row_count, model_width)
    first_of = jnp.arange(block_count, dtype=jnp.int32) - positions
    lower_rows, lower_cols = np.tril_indices(block_count)
    lower_rows = jnp.asarray(lower_rows, jnp.int32)
    lower_cols = jnp.asarray(lower_cols, jnp.int32)
    is_live = (first_of[lower_rows] == first_of[lower_cols]) & (lengths[lower_rows] > 0)
    order = jnp.argsort(jnp.where(is_live, 0, 1), stable=True)
    pair_query = lower_rows[order]
    pair_key = lower_cols[order]
    live_pairs = jnp.sum(is_live.astype(jnp.int32))

    def forward_step(step_index, attended):
        query_block = pair_query[step_index]
        key_block = pair_key[step_index]
        addend = pair_forward(
            pick(query_part, query_block),
            pick(key_part, key_block),
            pick(value_part, key_block),
            bias_table,
            pick(token_pos, query_block),
            pick(token_pos, key_block),
            pick(lengths, query_block),
        )
        return add_at(attended, query_block, addend)

    attended = lax.fori_loop(
        0, live_pairs, forward_step, jnp.zeros((block_count, row_count, model_width), jnp.float32)
    )
    att_n, att_inverse = norm_rows(attended.reshape(flat_rows, model_width))
    gate_float = gate_part.astype(jnp.float32)
    mixed = (att_n * gate_float).astype(jnp.bfloat16)
    upstream = jnp.where(valid, cot_blocks.reshape(flat_rows, model_width), 0)
    out_grad = jnp.einsum("td,te->de", mixed, upstream, preferred_element_type=jnp.float32)
    d_mixed = jnp.einsum("te,de->td", upstream, out_weight, preferred_element_type=jnp.float32)
    d_gate = d_mixed * att_n
    d_attended = norm_back(att_n, att_inverse, d_mixed * gate_float).astype(jnp.bfloat16)
    d_attended = d_attended.reshape(block_count, row_count, model_width)

    def backward_step(step_index, carry):
        d_query, d_key, d_value, d_table = carry
        query_block = pair_query[step_index]
        key_block = pair_key[step_index]
        grads = pair_backward(
            pick(query_part, query_block),
            pick(key_part, key_block),
            pick(value_part, key_block),
            pick(d_attended, query_block),
            bias_table,
            pick(token_pos, query_block),
            pick(token_pos, key_block),
            pick(lengths, query_block),
        )
        return (
            add_at(d_query, query_block, grads[0]),
            add_at(d_key, key_block, grads[1]),
            add_at(d_value, key_block, grads[2]),
            d_table + grads[3],
        )

    zero_blocks = jnp.zeros((block_count, row_count, model_width), jnp.float32)
    d_query, d_key, d_value, bias_grad = lax.fori_loop(
        0,
        live_pairs,
        backward_step,
        (zero_blocks, zero_blocks, zero_blocks, jnp.zeros((HEADS, BUCKETS), jnp.float32)),
    )
    d_acts = jnp.concatenate(
        [
            d_gate,
            d_value.reshape(flat_rows, model_width),
            d_query.reshape(flat_rows, model_width),
            d_key.reshape(flat_rows, model_width),
        ],
        axis=1,
    )
    d_proj = (d_acts * sigma * (1.0 + proj * (1.0 - sigma))).astype(jnp.bfloat16)
    proj_grad = jnp.einsum("td,tf->df", normed_b, d_proj, preferred_element_type=jnp.float32)
    d_normed = jnp.einsum("tf,df->td", d_proj, proj_weight, preferred_element_type=jnp.float32)
    token_grad = (upstream.astype(jnp.float32) + norm_back(normed, inverse, d_normed)).astype(
        jnp.bfloat16
    )
    return (token_grad, proj_grad, out_grad, bias_grad)


def shards(
    tokens,
    owner_cotangent,
    proj_weight,
    out_weight,
    bias_table,
    history_length,
    first_block,
    owner_slot,
):
    block_count = history_length.shape[0]
    model_width = tokens.shape[1]
    own_count = owner_cotangent.shape[0] // BLOCK
    loader_blocks = tokens.reshape(block_count, BLOCK, model_width)
    owner_blocks = owner_cotangent.reshape(own_count, BLOCK, model_width)
    positions = jnp.arange(block_count, dtype=jnp.int32) - first_block
    device_dp = lax.axis_index("dp")
    dp_count = lax.axis_size("dp")
    rep_count = lax.axis_size("rep")
    target_dp = owner_slot // own_count // rep_count
    offset_of = jnp.mod(target_dp - device_dp, dp_count)
    owner_place = owner_slot % own_count
    sub_slot = owner_place - jnp.where(offset_of == 0, 0, block_count + (offset_of - 1) * CAP)
    sub_starts = [0] + [block_count]
    sub_sizes = [block_count] + [CAP] * (REACH - 1)
    selectors = []
    for offset in range(REACH):
        slot_range = jnp.arange(sub_sizes[offset], dtype=jnp.int32)[:, None]
        selectors.append(
            ((offset_of[None, :] == offset) & (sub_slot[None, :] == slot_range)).astype(
                jnp.bfloat16
            )
        )
    block_meta = jnp.stack([history_length, positions], axis=1)
    sent_blocks = []
    sent_meta = []
    for offset in range(REACH):
        packed = jnp.einsum(
            "sb,btd->std", selectors[offset], loader_blocks, preferred_element_type=jnp.float32
        ).astype(jnp.bfloat16)
        packed_meta = jnp.sum(
            selectors[offset].astype(jnp.int32)[:, :, None] * block_meta[None, :, :], axis=1
        )
        if offset > 0:
            packed = passed_along(packed, "dp", offset)
            packed_meta = passed_along(packed_meta, "dp", offset)
        sent_blocks.append(packed)
        sent_meta.append(packed_meta)
    owner_rows = jnp.concatenate(sent_blocks, axis=0)
    owner_meta = jnp.concatenate(sent_meta, axis=0)
    owner_grad, proj_term, out_term, bias_term = layer_grads(
        owner_rows,
        owner_blocks,
        owner_meta[:, 0],
        owner_meta[:, 1],
        proj_weight,
        out_weight,
        bias_table,
    )
    owner_grad = owner_grad.reshape(own_count, BLOCK, model_width)
    returned = jnp.zeros((block_count, BLOCK, model_width), jnp.float32)
    for offset in range(REACH):
        piece_back = owner_grad[sub_starts[offset] : sub_starts[offset] + sub_sizes[offset]]
        if offset > 0:
            piece_back = passed_along(piece_back, "dp", -offset)
        returned = returned + jnp.einsum(
            "sb,std->btd", selectors[offset], piece_back, preferred_element_type=jnp.float32
        )
    token_grad = returned.astype(jnp.bfloat16).reshape(block_count * BLOCK, model_width)
    proj_grad = lax.psum_scatter(proj_term, ("dp", "rep"), scatter_dimension=1, tiled=True)
    out_grad, bias_grad = lax.psum((out_term, bias_term), ("dp", "rep"))
    return (token_grad, proj_grad, out_grad, bias_grad)


def solution(mesh):
    placed = (
        P(("dp", "rep"), None),
        P(("dp", "rep"), None),
        P(),
        P(),
        P(),
        P(("dp", "rep")),
        P(("dp", "rep")),
        P(("dp", "rep")),
    )
    return jax.shard_map(
        shards,
        mesh=mesh,
        in_specs=placed,
        out_specs=(P(("dp", "rep"), None), P(None, ("dp", "rep")), P(), P()),
        check_vma=False,
    )
```

profile of v0, /device:TPU:1, one launch (start us, length us, event | category | flops | bytes accessed | tf_op | source)
XLA Modules:
  0.0 835.0 jit_solution(13297879884279665192)
XLA Ops:
  8.8 1.5 convolution_convert_fusion.1
  10.3 5.4 collective-permute-start.1
  17.3 1.9 collective-permute-start
  19.2 1.7 convolution_convert_fusion
  21.3 1.9 collective-permute-done
  25.5 1.6 sort.17
  32.6 1.2 copy-done.4
  34.1 4.9 multiply_convert_fusion.3
  39.0 1.5 fusion.62
  41.2 2.3 copy.203
  43.5 2.3 copy.204
  45.8 1.2 copy.205
  47.0 1.2 broadcast.449
  48.2 75.1 %while.26 = (s32[]{:T(128)}, f32[6,128,512]{1,2,0:T(8,128)}, s32[]{:T(128)}, s32[21]{0:T(128)S(1)}, s32[21]{0:T(128)S(1)}, /*index=5*/bf16[6,128,512]{1,2,0:T(8,...) while((s32[]{:T(128)}, f32[6,128,512]{1,2,0:T(8,128)}, ...), condition=%wide.region_7.8_spmd, body=%wide.region_6.7_spmd.sunk | while | flops 42696968 | bytes 3020251 | solution.py:160
  55.8 1.0 constant_dynamic-slice_fusion.25
  58.9 1.7 constant_dynamic-update-slice_fusion.7
  68.2 1.0 constant_dynamic-slice_fusion.25
  71.3 1.7 constant_dynamic-update-slice_fusion.7
  80.6 1.0 constant_dynamic-slice_fusion.25
  83.7 1.7 constant_dynamic-update-slice_fusion.7
  96.1 1.7 constant_dynamic-update-slice_fusion.7
  108.5 1.7 constant_dynamic-update-slice_fusion.7
  117.8 1.0 constant_dynamic-slice_fusion.25
  120.9 1.7 constant_dynamic-update-slice_fusion.7
  123.4 3.0 copy.206
  126.4 1.6 reduce_sum.104
  128.0 1.7 multiply_reduce_fusion.3
  129.9 3.4 fusion.43
  133.4 2.8 multiply_convert_fusion.4
  136.2 1.3 broadcast.449.clone
  137.5 1.4 broadcast.449.clone2
  138.9 1.4 broadcast.449.clone2.1
  140.9 136.8 %while.27 = (s32[]{:T(128)}, f32[6,128,512]{2,1,0:T(8,128)}, f32[6,128,512]{2,1,0:T(8,128)}, f32[6,128,512]{2,1,0:T(8,128)}, f32[4,10]{1,0:T(4,128)}, /*index=5*...) while((s32[]{:T(128)}, f32[6,128,512]{2,1,0:T(8,128)}, ...), condition=%wide.region_13.14_spmd, body=%wide.region_12.13_spmd.sunk | while | flops 102039856 | bytes 19014368 | solution.py:195
  156.4 1.2 fusion.134
  179.0 1.2 fusion.134
  201.7 1.2 fusion.134
  224.4 1.2 fusion.134
  247.1 1.2 fusion.134
  269.9 1.2 fusion.134
  277.7 5.9 fusion.33
  283.7 3.8 fusion.63
  287.5 1.6 fusion.57
  289.8 4.4 fusion.59
  295.6 113.8 %collective-permute-start.2 = (bf16[2,128,512]{2,0,1:T(2,128)(2,1)S(1)}, bf16[2,128,512]{2,0,1:T(2,128)(2,1)S(1)}, u32[]{:S(2)}, u32[]{:S(2)}) collective-permute-start(bf16[2,128,512]{2,0,1:T(2,128)(2,1)S(1)} %copy.215), channel_id=1, source_target_pairs={{0,508},{4,0},{8,4},{12,8},{16,12},{20,16},{24,20},{28,24},{32,28}... | collective-permute-start | bytes 786440 | tf_op jit(solution)/shard_map/ppermute | solution.py:21
  409.4 236.0 %psum.15 = f32[4,10]{1,0:T(4,128)} all-reduce(f32[4,10]{1,0:T(4,128)S(1)} %copy-done.27), channel_id=1, replica_groups=mesh['dp'=128,'rep'=4] {'dp','rep'}, use_global_device_ids=true, to_apply=%region_18.19 | all-reduce | flops 40 | bytes 320 | tf_op jit(solution)/shard_map/psum | solution.py:289
  647.5 177.1 %all-reduce.4.cloned.1.call-done = (f32[512,2048]{0,1:T(8,128)}, f32[512,512]{1,0:T(8,128)}) async-done(((f32[512,2048]{0,1:T(8,128)}, f32[512,512]{1,0:T(8,128)}), (f32[512,2048]{0,1:T(8,128)}, f32[512,512]{1,0:T(8,128)})) %all-reduce.4.cloned.1.call-update) | async-done | bytes 5242896
  824.5 1.3 constant_dynamic-slice_fusion.14
  825.9 2.3 copy.304
  (534 shorter events, 148.9 us)
Async XLA Ops:
  7.2 26.9 %copy-start = (bf16[512,2048]{1,0:T(8,128)(2,1)S(1)}, bf16[512,2048]{1,0:T(8,128)(2,1)}, u32[]{:S(2)}) copy-start(bf16[512,2048]{1,0:T(8,128)(2,1)} %param.16) | copy-start | bytes 6291460
  7.2 14.1 %copy-start.2 = (s32[21]{0:T(128)S(1)}, s32[21]{0:T(128)}, u32[]{:S(2)}) copy-start(s32[21]{0:T(128)} %constant.202.clone) | copy-start | bytes 256
  7.2 14.1 %copy-start.1 = (s32[21]{0:T(128)S(1)}, s32[21]{0:T(128)}, u32[]{:S(2)}) copy-start(s32[21]{0:T(128)} %constant.203.clone) | copy-start | bytes 256
  7.2 817.3 %all-reduce.4.cloned.1.call-start = ((), (), s32[]{:S(2)}) async-start(), calls=%async_computation | async-start | bytes 10485760
  8.1 13.2 %copy-start.30 = (pred[4]{0:T(512)(128)(4,1)}, pred[4]{0:T(512)(128)(4,1)S(1)}, u32[]{:S(2)}) copy-start(pred[4]{0:T(512)(128)(4,1)S(1)} %get-tuple-element.355) | copy-start | bytes 16
  8.8 12.3 %copy-start.28 = (s32[4]{0:T(128)}, s32[4]{0:T(128)S(1)}, u32[]{:S(2)}) copy-start(s32[4]{0:T(128)S(1)} %fusion.51) | copy-start | bytes 52
  8.8 7.6 copy-start.32
  10.3 19.0 %collective-permute-start.1 = (bf16[2,128,512]{2,0,1:T(2,128)(2,1)S(1)}, bf16[2,128,512]{2,0,1:T(2,128)(2,1)S(1)}, u32[]{:S(2)}, u32[]{:S(2)}) collective-permute-start(bf16[2,128,512]{2,0,1:T(2,128)(2,1)S(1)} %convolution_convert_fusion.1), channel_id=1, source_target_pairs={{0,4},{4,8},{8,12},{12,16},{16,20},{20,24},{24,28},{28,32},{32,36}... | collective-permute-start | bytes 786440 | tf_op jit(solution)/shard_map/ppermute | solution.py:21
  17.3 5.9 collective-permute-start
  27.2 102.6 %copy-start.23 = (pred[768]{0:T(1024)(128)(4,1)}, pred[768]{0:T(1024)(128)(4,1)S(1)}, u32[]{:S(2)}) copy-start(pred[768]{0:T(1024)(128)(4,1)S(1)} %compare_bitcast_fusion.2) | copy-start | bytes 2308
  34.1 5.0 copy-start.17
  126.4 3.3 copy-start.12
  126.4 3.3 copy-start.19
  141.5 12.4 %copy-start.34 = (s32[21]{0:T(128)}, s32[21]{0:T(128)S(1)}, u32[]{:S(2)}) copy-start(s32[21]{0:T(128)S(1)} %get-tuple-element.643) | copy-start | bytes 256 | tf_op jit(solution)/shard_map/while
  141.5 12.4 %copy-start.36 = (s32[21]{0:T(128)}, s32[21]{0:T(128)S(1)}, u32[]{:S(2)}) copy-start(s32[21]{0:T(128)S(1)} %get-tuple-element.644) | copy-start | bytes 256 | tf_op jit(solution)/shard_map/while
  151.0 2.9 copy-start.7
  164.2 12.4 %copy-start.34 = (s32[21]{0:T(128)}, s32[21]{0:T(128)S(1)}, u32[]{:S(2)}) copy-start(s32[21]{0:T(128)S(1)} %get-tuple-element.643) | copy-start | bytes 256 | tf_op jit(solution)/shard_map/while
  164.2 12.4 %copy-start.36 = (s32[21]{0:T(128)}, s32[21]{0:T(128)S(1)}, u32[]{:S(2)}) copy-start(s32[21]{0:T(128)S(1)} %get-tuple-element.644) | copy-start | bytes 256 | tf_op jit(solution)/shard_map/while
  173.7 2.9 copy-start.7
  183.6 2.6 copy-start.35
  183.6 2.6 copy-start.37
  186.9 12.4 %copy-start.34 = (s32[21]{0:T(128)}, s32[21]{0:T(128)S(1)}, u32[]{:S(2)}) copy-start(s32[21]{0:T(128)S(1)} %get-tuple-element.643) | copy-start | bytes 256 | tf_op jit(solution)/shard_map/while
  186.9 12.4 %copy-start.36 = (s32[21]{0:T(128)}, s32[21]{0:T(128)S(1)}, u32[]{:S(2)}) copy-start(s32[21]{0:T(128)S(1)} %get-tuple-element.644) | copy-start | bytes 256 | tf_op jit(solution)/shard_map/while
  196.4 2.9 copy-start.7
  206.3 2.6 copy-start.35
  209.6 12.4 %copy-start.34 = (s32[21]{0:T(128)}, s32[21]{0:T(128)S(1)}, u32[]{:S(2)}) copy-start(s32[21]{0:T(128)S(1)} %get-tuple-element.643) | copy-start | bytes 256 | tf_op jit(solution)/shard_map/while
  209.6 12.4 %copy-start.36 = (s32[21]{0:T(128)}, s32[21]{0:T(128)S(1)}, u32[]{:S(2)}) copy-start(s32[21]{0:T(128)S(1)} %get-tuple-element.644) | copy-start | bytes 256 | tf_op jit(solution)/shard_map/while
  219.1 2.9 copy-start.7
  229.0 2.6 copy-start.35
  232.3 12.4 %copy-start.34 = (s32[21]{0:T(128)}, s32[21]{0:T(128)S(1)}, u32[]{:S(2)}) copy-start(s32[21]{0:T(128)S(1)} %get-tuple-element.643) | copy-start | bytes 256 | tf_op jit(solution)/shard_map/while
  232.3 12.4 %copy-start.36 = (s32[21]{0:T(128)}, s32[21]{0:T(128)S(1)}, u32[]{:S(2)}) copy-start(s32[21]{0:T(128)S(1)} %get-tuple-element.644) | copy-start | bytes 256 | tf_op jit(solution)/shard_map/while
  241.8 2.9 copy-start.7
  251.8 2.6 copy-start.35
  255.0 12.4 %copy-start.34 = (s32[21]{0:T(128)}, s32[21]{0:T(128)S(1)}, u32[]{:S(2)}) copy-start(s32[21]{0:T(128)S(1)} %get-tuple-element.643) | copy-start | bytes 256 | tf_op jit(solution)/shard_map/while
  255.0 12.4 %copy-start.36 = (s32[21]{0:T(128)}, s32[21]{0:T(128)S(1)}, u32[]{:S(2)}) copy-start(s32[21]{0:T(128)S(1)} %get-tuple-element.644) | copy-start | bytes 256 | tf_op jit(solution)/shard_map/while
  264.5 2.9 copy-start.7
  274.4 2.6 copy-start.35
  277.7 5.9 copy-start.18
  283.6 3.9 copy-start.14
  283.6 3.9 copy-start.13
  283.6 3.9 copy-start.16
  283.6 3.8 copy-start.24
  289.8 4.4 copy-start.5
  295.2 114.2 %copy-start.27 = (f32[4,10]{1,0:T(4,128)S(1)}, f32[4,10]{1,0:T(4,128)}, u32[]{:S(2)}) copy-start(f32[4,10]{1,0:T(4,128)} %get-tuple-element.149) | copy-start | bytes 484
  295.2 350.2 %copy-start.29 = (s32[4]{0:T(128)S(1)}, s32[4]{0:T(128)}, u32[]{:S(2)}) copy-start(s32[4]{0:T(128)} %copy-done.28) | copy-start | bytes 52
  295.2 350.2 %copy-start.31 = (pred[4]{0:T(512)(128)(4,1)S(1)}, pred[4]{0:T(512)(128)(4,1)}, u32[]{:S(2)}) copy-start(pred[4]{0:T(512)(128)(4,1)} %copy-done.30) | copy-start | bytes 16
  295.3 350.7 %copy-start.33 = (pred[4]{0:T(512)(128)(4,1)S(1)}, pred[4]{0:T(512)(128)(4,1)}, u32[]{:S(2)}) copy-start(pred[4]{0:T(512)(128)(4,1)} %copy-done.32) | copy-start | bytes 16
  295.6 350.4 %collective-permute-start.2 = (bf16[2,128,512]{2,0,1:T(2,128)(2,1)S(1)}, bf16[2,128,512]{2,0,1:T(2,128)(2,1)S(1)}, u32[]{:S(2)}, u32[]{:S(2)}) collective-permute-start(bf16[2,128,512]{2,0,1:T(2,128)(2,1)S(1)} %copy.215), channel_id=1, source_target_pairs={{0,508},{4,0},{8,4},{12,8},{16,12},{20,16},{24,20},{28,24},{32,28}... | collective-permute-start | bytes 786440 | tf_op jit(solution)/shard_map/ppermute | solution.py:21
  (54 other events, 87.1 us)
Sparse Core Ops, SparseCore 0:
  289.3 535.2 all-reduce.3
where the time goes:
time: 842 us; the launch traced here: 835 us
  blocking collectives  236 us (28%)
  waiting for transfers between devices  179 us (21%)
  local copies, waits for them, and re-layouts  127 us (15%)
  starting transfers between devices  121 us (14%)
  loops' own time  58.3 us (7%)
  other arithmetic  50 us (6%)
  matrix products  48.8 us (6%)
  between operations  14.5 us (2%)
    psum x1, blocking collectives, shards(): out_grad, bias_grad = lax.psum((out_term, bias_term), ('dp', 'rep'))  236 us
    unnamed x2, waiting for transfers between devices  177 us
    ppermute x3, starting transfers between devices, passed_along(): return lax.ppermute(value, axis, pairs)  121 us
    dynamic_slice x96, local copies, waits for them, and re-layouts, pick(): return lax.dynamic_index_in_dim(stacked, where_at, 0, keepdims=False)  62.2 us
    another operation x1, loops' own time, layer_grads(): lax.fori_loop(0, live_pairs, backward_step, (zero_blocks, zero_blocks, ze...  30 us
    another operation x1, loops' own time, layer_grads(): lax.fori_loop(0, live_pairs, forward_step, jnp.zeros((block_count, row_co...  28.4 us
  transfers between devices with their start and end apart: 4, of which 2 were waited for; matrix products, arithmetic and copies ran while one was open for 2% of the time, Pallas kernels for 0%

commit v1 on v0

v1 whole, which is shorter than its diff:
```python
import jax
import jax.numpy as jnp
from jax import lax
from jax.experimental import pallas as pl
from jax.experimental.pallas import tpu as pltpu
from jax.sharding import PartitionSpec as P

HEADS = 4
HEAD_DIM = 128
BLOCK = 128
BLOCKS = 4
SLOTS = 6
BUCKETS = 10
D = 512
ROWS = BLOCKS * BLOCK
EPSILON = 1e-06
SCALE = HEAD_DIM ** (-0.5)
BF16 = jnp.bfloat16
F32 = jnp.float32
BUCKETS_AT = (range(0, 8), range(1, 9), range(8, 10), range(9, 10))


def dot(a, b):
    return lax.dot_general(a, b, (((1,), (0,)), ((), ())), preferred_element_type=F32)


def dot_right_t(a, b):
    return lax.dot_general(a, b, (((1,), (1,)), ((), ())), preferred_element_type=F32)


def dot_left_t(a, b):
    return lax.dot_general(a, b, (((0,), (0,)), ((), ())), preferred_element_type=F32)


def row_sum(parts):
    total = parts[0]
    for part in parts[1:]:
        total = total + part
    return jnp.sum(total, axis=-1, keepdims=True)


def tile_iota(axis):
    return lax.broadcasted_iota(jnp.int32, (BLOCK, BLOCK), axis)


def norm_tokens(tokens_ref, normed_ref, normed_b_ref, inverse_ref):
    def body(b, carry):
        rows = pl.ds(pl.multiple_of(b * BLOCK, BLOCK), BLOCK)
        x = tokens_ref[rows, :].astype(F32)
        centered = x - jnp.mean(x, axis=-1, keepdims=True)
        inverse = lax.rsqrt(jnp.mean(centered * centered, axis=-1, keepdims=True) + EPSILON)
        normed = centered * inverse
        normed_ref[rows, :] = normed
        normed_b_ref[rows, :] = normed.astype(BF16)
        inverse_ref[rows, :] = jnp.broadcast_to(inverse, (BLOCK, BLOCK))
        return carry

    lax.fori_loop(0, BLOCKS, body, 0)


def project(normed_b_ref, weight_ref, acts_ref, slope_ref):
    def body(c, carry):
        columns = pl.ds(pl.multiple_of(c * 256, 256), 256)
        half = dot(normed_b_ref[...], weight_ref[:, columns]) * 0.5
        u = 1.0 + jnp.tanh(half)
        act = half * u
        slope = 0.5 * (u + act * (2.0 - u))
        act = act.astype(BF16)
        for k in range(2):
            acts_ref[2 * c + k] = act[:, k * 128 : (k + 1) * 128]
            slope_ref[2 * c + k] = slope[:, k * 128 : (k + 1) * 128]
        return carry

    lax.fori_loop(0, 8, body, 0)


def take_upstream(own_ref, received_ref, slot_ref, length_ref, first_ref, upstream_ref):
    def body(b, carry):
        rows = pl.ds(pl.multiple_of(b * BLOCK, BLOCK), BLOCK)
        slot = lax.rem(slot_ref[b], SLOTS)
        own_at = pl.multiple_of(jnp.minimum(slot, 3) * BLOCK, BLOCK)
        received_at = pl.multiple_of(jnp.maximum(slot - 4, 0) * BLOCK, BLOCK)
        own = own_ref[pl.ds(own_at, BLOCK), :].astype(F32)
        received = received_ref[pl.ds(received_at, BLOCK), :].astype(F32)
        limit = length_ref[b] - (b - first_ref[b]) * BLOCK
        row = lax.broadcasted_iota(jnp.int32, (BLOCK, D), 0)
        is_own = jnp.full((BLOCK, D), slot, jnp.int32) < 4
        value = jnp.where(row < limit, jnp.where(is_own, own, received), 0.0)
        upstream_ref[rows, :] = value.astype(BF16)
        return carry

    lax.fori_loop(0, BLOCKS, body, 0)


def mix_back(upstream_ref, out_weight_ref, d_mixed_ref):
    for c in range(2):
        part = dot_right_t(upstream_ref[...], out_weight_ref[c * 256 : (c + 1) * 256, :])
        for k in range(2):
            d_mixed_ref[2 * c + k] = part[:, k * 128 : (k + 1) * 128]


def bucket_bounds(apart):
    distance = tile_iota(0) - tile_iota(1) + apart * BLOCK
    return distance, [(bucket, 0 if bucket == 0 else 2 ** (bucket - 1)) for bucket in BUCKETS_AT[apart]]


def bias_tiles(table_ref, head):
    tiles = []
    for apart in range(BLOCKS):
        distance, bounds = bucket_bounds(apart)
        tile = jnp.full((BLOCK, BLOCK), table_ref[head, bounds[0][0]] * 0.5, F32)
        for bucket, least in bounds[1:]:
            tile = jnp.where(distance >= least, table_ref[head, bucket] * 0.5, tile)
        tiles.append(tile)
    return tiles


def attend(acts_ref, table_ref, length_ref, first_ref, weights_ref, factor_ref, attended_ref):
    def body(head, carry):
        bias = bias_tiles(table_ref, head)
        row = tile_iota(0)
        causal_row = jnp.where(tile_iota(1) <= row, row, ROWS)
        for i in range(BLOCKS):
            rows = pl.ds(i * BLOCK, BLOCK)
            upto = (i + 1) * BLOCK
            scores = dot_right_t(acts_ref[8 + head, rows, :], acts_ref[12 + head, 0:upto, :])
            for j in range(i + 1):
                lanes = pl.ds(j * BLOCK, BLOCK)
                limit = jnp.where(
                    first_ref[i] == first_ref[j], length_ref[i] - (i - first_ref[i]) * BLOCK, 0
                )
                half = scores[:, j * BLOCK : (j + 1) * BLOCK] * (0.5 * SCALE) + bias[i - j]
                kept = (causal_row if i == j else row) < limit
                u = jnp.where(kept, 1.0 + jnp.tanh(half), 0.0)
                weight = half * u
                factor_ref[head, rows, lanes] = 0.5 * (u + weight * (2.0 - u))
                weights_ref[head, rows, lanes] = weight.astype(BF16)
            attended_ref[head, rows, :] = dot(
                weights_ref[head, rows, 0:upto], acts_ref[4 + head, 0:upto, :]
            )
        return carry

    lax.fori_loop(0, HEADS, body, 0)


def mix(acts_ref, attended_ref, d_mixed_ref, slope_ref, mixed_ref, d_attended_ref, d_proj_ref):
    def body(b, carry):
        rows = pl.ds(pl.multiple_of(b * BLOCK, BLOCK), BLOCK)
        heads = range(HEADS)
        att = [attended_ref[h, rows, :] for h in heads]
        mean = row_sum(att) * (1.0 / D)
        centered = [a - mean for a in att]
        inverse = lax.rsqrt(row_sum([c * c for c in centered]) * (1.0 / D) + EPSILON)
        normed = [c * inverse for c in centered]
        gate = [acts_ref[h, rows, :].astype(F32) for h in heads]
        d_mixed = [d_mixed_ref[h, rows, :] for h in heads]
        g = [d_mixed[h] * gate[h] for h in heads]
        g_mean = row_sum(g) * (1.0 / D)
        g_dot = row_sum([g[h] * normed[h] for h in heads]) * (1.0 / D)
        for h in heads:
            lanes = pl.ds(h * 128, 128)
            mixed_ref[rows, lanes] = (normed[h] * gate[h]).astype(BF16)
            d_attended_ref[h, rows, :] = (inverse * (g[h] - g_mean - normed[h] * g_dot)).astype(BF16)
            d_proj_ref[rows, lanes] = (d_mixed[h] * normed[h] * slope_ref[h, rows, :]).astype(BF16)
        return carry

    lax.fori_loop(0, BLOCKS, body, 0)


def attend_back(
    acts_ref, weights_ref, factor_ref, d_attended_ref, slope_ref, d_logits_ref, d_proj_ref, bias_ref
):
    def body(head, carry):
        sums = [None] * BLOCKS
        for i in range(BLOCKS):
            rows = pl.ds(i * BLOCK, BLOCK)
            upto = (i + 1) * BLOCK
            d_weights = dot_right_t(d_attended_ref[head, rows, :], acts_ref[4 + head, 0:upto, :])
            for j in range(i + 1):
                lanes = pl.ds(j * BLOCK, BLOCK)
                d_logits = d_weights[:, j * BLOCK : (j + 1) * BLOCK] * factor_ref[head, rows, lanes]
                sums[i - j] = d_logits if sums[i - j] is None else sums[i - j] + d_logits
                d_logits_ref[rows, lanes] = d_logits.astype(BF16)
            d_query = dot(d_logits_ref[rows, 0:upto], acts_ref[12 + head, 0:upto, :])
            at = pl.ds(pl.multiple_of(1024 + head * 128, 128), 128)
            d_proj_ref[rows, at] = (d_query * SCALE * slope_ref[8 + head, rows, :]).astype(BF16)
        for j in range(BLOCKS):
            rows = pl.ds(j * BLOCK, BLOCK)
            below = pl.ds(j * BLOCK, ROWS - j * BLOCK)
            d_value = dot_left_t(weights_ref[head, below, rows], d_attended_ref[head, below, :])
            at = pl.ds(pl.multiple_of(512 + head * 128, 128), 128)
            d_proj_ref[rows, at] = (d_value * slope_ref[4 + head, rows, :]).astype(BF16)
            d_key = dot_left_t(d_logits_ref[below, rows], acts_ref[8 + head, below, :])
            at = pl.ds(pl.multiple_of(1536 + head * 128, 128), 128)
            d_proj_ref[rows, at] = (d_key * SCALE * slope_ref[12 + head, rows, :]).astype(BF16)
        totals = [None] * BUCKETS
        for apart in range(BLOCKS):
            distance, bounds = bucket_bounds(apart)
            for at, (bucket, least) in enumerate(bounds):
                value = sums[apart]
                if at > 0:
                    value = jnp.where(distance >= least, value, 0.0)
                if at + 1 < len(bounds):
                    value = jnp.where(distance < bounds[at + 1][1], value, 0.0)
                value = jnp.sum(value, axis=0, keepdims=True)
                totals[bucket] = value if totals[bucket] is None else totals[bucket] + value
        lane = lax.broadcasted_iota(jnp.int32, (1, 128), 1)
        packed = jnp.zeros((1, 128), F32)
        for bucket in range(BUCKETS):
            packed = jnp.where(lane == bucket, jnp.sum(totals[bucket], axis=1, keepdims=True), packed)
        bias_ref[pl.ds(head, 1), :] = packed
        return carry

    lax.fori_loop(0, HEADS, body, 0)


def weight_grads(normed_b_ref, d_proj_ref, proj_term_ref):
    def body(c, carry):
        at = pl.ds(pl.multiple_of(c * 256, 256), 256)
        proj_term_ref[at, :] = dot_left_t(d_proj_ref[:, at], normed_b_ref[...]).astype(
            proj_term_ref.dtype
        )
        return carry

    lax.fori_loop(0, 8, body, 0)


def token_grads(d_proj_ref, weight_ref, normed_ref, inverse_ref, upstream_ref, token_grad_ref):
    def body(b, carry):
        rows = pl.ds(pl.multiple_of(b * 256, 256), 256)
        d_normed = dot_right_t(d_proj_ref[rows, :], weight_ref[...])
        normed = normed_ref[rows, :]
        inverse = inverse_ref[rows, 0:1]
        mean = jnp.mean(d_normed, axis=-1, keepdims=True)
        along = jnp.mean(d_normed * normed, axis=-1, keepdims=True)
        back = inverse * (d_normed - mean - normed * along)
        token_grad_ref[rows, :] = (upstream_ref[rows, :].astype(F32) + back).astype(BF16)
        return carry

    lax.fori_loop(0, 2, body, 0)


def layer_kernel(
    tokens_ref,
    own_ref,
    received_ref,
    weight_ref,
    out_weight_ref,
    table_ref,
    length_ref,
    first_ref,
    slot_ref,
    token_grad_ref,
    proj_term_ref,
    out_term_ref,
    bias_ref,
    normed_ref,
    normed_b_ref,
    inverse_ref,
    acts_ref,
    slope_ref,
    upstream_ref,
    d_mixed_ref,
    weights_ref,
    factor_ref,
    attended_ref,
    mixed_ref,
    d_attended_ref,
    d_logits_ref,
    d_proj_ref,
):
    norm_tokens(tokens_ref, normed_ref, normed_b_ref, inverse_ref)
    project(normed_b_ref, weight_ref, acts_ref, slope_ref)
    attend(acts_ref, table_ref, length_ref, first_ref, weights_ref, factor_ref, attended_ref)
    take_upstream(own_ref, received_ref, slot_ref, length_ref, first_ref, upstream_ref)
    mix_back(upstream_ref, out_weight_ref, d_mixed_ref)
    mix(acts_ref, attended_ref, d_mixed_ref, slope_ref, mixed_ref, d_attended_ref, d_proj_ref)
    out_term_ref[...] = dot_left_t(mixed_ref[...], upstream_ref[...]).astype(out_term_ref.dtype)
    bias_ref[...] = jnp.zeros_like(bias_ref)
    attend_back(
        acts_ref, weights_ref, factor_ref, d_attended_ref, slope_ref, d_logits_ref, d_proj_ref, bias_ref
    )
    weight_grads(normed_b_ref, d_proj_ref, proj_term_ref)
    token_grads(d_proj_ref, weight_ref, normed_ref, inverse_ref, upstream_ref, token_grad_ref)


LAYER_SCRATCH = [
    pltpu.VMEM((ROWS, D), F32),
    pltpu.VMEM((ROWS, D), BF16),
    pltpu.VMEM((ROWS, BLOCK), F32),
    pltpu.VMEM((16, ROWS, 128), BF16),
    pltpu.VMEM((16, ROWS, 128), F32),
    pltpu.VMEM((ROWS, D), BF16),
    pltpu.VMEM((HEADS, ROWS, 128), F32),
    pltpu.VMEM((HEADS, ROWS, ROWS), BF16),
    pltpu.VMEM((HEADS, ROWS, ROWS), F32),
    pltpu.VMEM((HEADS, ROWS, 128), F32),
    pltpu.VMEM((ROWS, D), BF16),
    pltpu.VMEM((HEADS, ROWS, 128), BF16),
    pltpu.VMEM((ROWS, ROWS), BF16),
    pltpu.VMEM((ROWS, 4 * D), BF16),
]


def layer_grads(tokens, own, received, weight, out_weight, table, length, first, slot, term_type):
    vmem = pl.BlockSpec(memory_space=pltpu.VMEM)
    smem = pl.BlockSpec(memory_space=pltpu.SMEM)
    return pl.pallas_call(
        layer_kernel,
        out_shape=(
            jax.ShapeDtypeStruct((ROWS, D), BF16),
            jax.ShapeDtypeStruct((4 * D, D), term_type),
            jax.ShapeDtypeStruct((D, D), term_type),
            jax.ShapeDtypeStruct((8, 128), F32),
        ),
        in_specs=[vmem] * 5 + [smem] * 4,
        out_specs=(vmem,) * 4,
        scratch_shapes=LAYER_SCRATCH,
        compiler_params=pltpu.CompilerParams(vmem_limit_bytes=52 * 2**20),
        name="layer_grads",
    )(tokens, own, received, weight, out_weight, table, length, first, slot)


def shards(tokens, cotangent, weight, out_weight, table, length, first, slot):
    count = lax.axis_size("dp")
    received = lax.ppermute(
        cotangent[ROWS:], "dp", [(source, (source - 1) % count) for source in range(count)]
    )
    token_grad, proj_term, out_term, bias_term = layer_grads(
        tokens, cotangent, received, weight, out_weight, table, length, first, slot, F32
    )
    proj_grad = lax.psum_scatter(proj_term, ("dp", "rep"), scatter_dimension=0, tiled=True)
    out_grad, bias_grad = lax.psum((out_term, bias_term), ("dp", "rep"))
    return token_grad, proj_grad.T, out_grad, bias_grad[:HEADS, :BUCKETS]


def solution(mesh):
    split = P(("dp", "rep"))
    return jax.shard_map(
        shards,
        mesh=mesh,
        in_specs=(split, split, P(), P(), P(), split, split, split),
        out_specs=(split, P(None, ("dp", "rep")), P(), P()),
        check_vma=False,
    )
```

time: 842 us -> 350 us (0.42)
  blocking collectives: 236 us -> 109 us
  local copies, waits for them, and re-layouts: 127 us -> 9.86 us
  starting transfers between devices: 121 us -> 8.82 us
  loops' own time: 58.3 us -> 0 us
  other arithmetic: 50 us -> 0 us
  matrix products: 48.8 us -> 0 us
  Pallas kernels: 0 us -> 21.9 us
    psum x1, blocking collectives: 236 us -> 109 us  [shards(): out_grad, bias_grad = lax.psum((out_term, bias_term), ('dp', 'rep'))]
    ppermute x3 -> x1, starting transfers between devices: 121 us -> 8.79 us  [shards(): lax.ppermute(cotangent[ROWS:], 'dp', [(source, (source - 1) % count) for...]
    dynamic_slice x120 -> x0, local copies, waits for them, and re-layouts: 76.3 us -> none  [the longest x96 62.2 us: pick(): return lax.dynamic_index_in_dim(stacked, where_at, 0, keepdims=False)]
    another operation x2 -> x0, loops' own time: 58.3 us -> none  [the longest x1 30 us: layer_grads(): lax.fori_loop(0, live_pairs, backward_step, (zero_blocks, zero_blocks, ze...]
    dot_general x63 -> x0, matrix products: 48.8 us -> none  [the longest x6 7.45 us: pair_backward(): jnp.einsum('hqk,qhd->khd', weights, upstream_heads, preferred_element_typ...]
    pallas_call x0 -> x1, Pallas kernels: none -> 21.9 us  [layer_grads(): pl.pallas_call(layer_kernel, out_shape=(jax.ShapeDtypeStruct((ROWS, D), B...]
    dynamic_update_slice x30 -> x0, local copies, waits for them, and re-layouts: 16 us -> none  [add_at(): lax.dynamic_update_index_in_dim(stacked, pick(stacked, where_at) + addend...]
    lt x25 -> x0, other arithmetic: 15.8 us -> none  [the longest x12 7.88 us: pair_logits(): key_pos[None, :] < seq_length]
  transfers between devices with their start and end apart: 4 -> 2, of which waited for: 2 -> 2; matrix products, arithmetic and copies ran while one was open for 2% -> 0% of each run, Pallas kernels for 0% -> 0%
where the time goes in v1:
time: 350 us; the launch traced here: 348 us
  waiting for transfers between devices  185 us (53%)
  blocking collectives  109 us (31%)
  Pallas kernels  21.9 us (6%)
  between operations  14.1 us (4%)
  local copies, waits for them, and re-layouts  9.86 us (3%)
  starting transfers between devices  8.82 us (3%)
    unnamed x2, waiting for transfers between devices  184 us
    psum x1, blocking collectives, shards(): out_grad, bias_grad = lax.psum((out_term, bias_term), ('dp', 'rep'))  109 us
    pallas_call x1, Pallas kernels, layer_grads(): pl.pallas_call(layer_kernel, out_shape=(jax.ShapeDtypeStruct((ROWS, D), B...  21.9 us
    ppermute x1, starting transfers between devices, shards(): lax.ppermute(cotangent[ROWS:], 'dp', [(source, (source - 1) % count) for...  8.79 us
  transfers between devices with their start and end apart: 2, of which 2 were waited for; matrix products, arithmetic and copies ran while one was open for 0% of the time, Pallas kernels for 0%

profile of v1, /device:TPU:1, one launch (start us, length us, event | category | flops | bytes accessed | tf_op | source)
XLA Modules:
  0.0 348.5 jit_solution(17866636730238747407)
XLA Ops:
  7.2 0.0 all-reduce.4.cloned.1.call-start
  7.2 1.0 slice.6
  8.2 8.8 %collective-permute-start = (bf16[256,512]{1,0:T(8,128)(2,1)S(1)}, bf16[256,512]{1,0:T(8,128)(2,1)S(1)}, u32[]{:S(2)}, u32[]{:S(2)}) collective-permute-start(bf16[256,512]{1,0:T(8,128)(2,1)S(1)} %slice.6), channel_id=1, source_target_pairs={{0,508},{4,0},{8,4},{12,8},{16,12},{20,16},{24,20},{28,24},{32,28}... | collective-permute-start | bytes 786440 | tf_op jit(solution)/shard_map/ppermute | solution.py:326
  17.0 1.1 collective-permute-done.received_ref
  18.1 0.0 copy-start
  18.1 1.0 copy-done
  19.2 0.0 copy-start.1
  19.2 1.0 copy-done.1
  20.2 0.0 copy-start.2
  20.2 0.7 copy-done.2
  20.9 0.0 copy-start.3
  20.9 0.7 copy-done.3
  21.5 0.0 copy-start.4
  21.5 0.7 copy-done.4
  22.2 0.0 copy-start.5
  22.2 0.7 copy-done.5
  22.9 21.9 %layer_grads.1 = (bf16[512,512]{1,0:T(8,128)(2,1)}, f32[2048,512]{1,0:T(8,128)}, f32[512,512]{1,0:T(8,128)}, f32[8,128]{1,0:T(8,128)S(1)}) custom-call(bf16[512,512]{1,0:T(8,128)(2,1)S(1)} %copy-done, bf16[768,512]{1,0:T(8,128)(2,1)} %own_ref.1, bf16[256,512]{1,0:T(8,128)(2,1)S(1)} %collective-permute-done.received_ref, bf16[512,2048]{1,0:T(8,128)(2,1)} %weight_ref.1, ...), custom_call_target="tpu_custom_call" | custom-call | tf_op jit(solution)/shard_map/layer_grads/pallas_call | solution.py:308
  44.8 0.0 all-reduce.4.cloned.1.call-update
  44.8 108.6 %psum.15 = f32[8,128]{1,0:T(8,128)S(1)} all-reduce(f32[8,128]{1,0:T(8,128)S(1)} %get-tuple-element.11), channel_id=1, replica_groups=mesh['dp'=128,'rep'=4] {'dp','rep'}, use_global_device_ids=true, to_apply=%region_2.0 | all-reduce | flops 1024 | bytes 8192 | tf_op jit(solution)/shard_map/psum | solution.py:333
  153.5 0.6 slice.7
  154.0 184.0 %all-reduce.4.cloned.1.call-done = (f32[2048,512]{1,0:T(8,128)}, f32[512,512]{1,0:T(8,128)}) async-done(((f32[2048,512]{1,0:T(8,128)}, f32[512,512]{1,0:T(8,128)}), (f32[2048,512]{1,0:T(8,128)}, f32[512,512]{1,0:T(8,128)})) %all-reduce.4.cloned.1.call-update) | async-done | bytes 5242896
  338.1 1.3 dynamic-slice_bitcast_fusion
  339.4 2.3 copy.14
Async XLA Ops:
  7.2 330.9 %all-reduce.4.cloned.1.call-start = ((), (), s32[]{:S(2)}) async-start(), calls=%async_computation | async-start | bytes 10485760
  8.2 9.9 %collective-permute-start = (bf16[256,512]{1,0:T(8,128)(2,1)S(1)}, bf16[256,512]{1,0:T(8,128)(2,1)S(1)}, u32[]{:S(2)}, u32[]{:S(2)}) collective-permute-start(bf16[256,512]{1,0:T(8,128)(2,1)S(1)} %slice.6), channel_id=1, source_target_pairs={{0,508},{4,0},{8,4},{12,8},{16,12},{20,16},{24,20},{28,24},{32,28}... | collective-permute-start | bytes 786440 | tf_op jit(solution)/shard_map/ppermute | solution.py:326
  18.1 1.0 copy-start
  19.2 1.0 copy-start.1
  20.2 0.7 copy-start.2
  20.9 0.7 copy-start.3
  21.5 0.7 copy-start.4
  22.2 0.7 copy-start.5
Sparse Core Ops, SparseCore 0:
  44.9 293.0 all-reduce.3

commit v2 on v1

v2 whole, which is shorter than its diff:
```python
import jax
import jax.numpy as jnp
from jax import lax
from jax.experimental import pallas as pl
from jax.experimental.pallas import tpu as pltpu
from jax.sharding import PartitionSpec as P

HEADS = 4
HEAD_DIM = 128
BLOCK = 128
BLOCKS = 4
SLOTS = 6
BUCKETS = 10
NX, NY, NZ = 4, 8, 8
SETS = HEADS + 1
D = 512
ROWS = BLOCKS * BLOCK
EPSILON = 1e-06
SCALE = HEAD_DIM ** (-0.5)
BF16 = jnp.bfloat16
F32 = jnp.float32
GATE, VALUE, QUERY, KEY = (slice(g * 128, (g + 1) * 128) for g in range(4))
BUCKETS_AT = (range(0, 8), range(1, 9), range(8, 10), range(9, 10))


def dot(a, b):
    return lax.dot_general(a, b, (((1,), (0,)), ((), ())), preferred_element_type=F32)


def dot_right_t(a, b):
    return lax.dot_general(a, b, (((1,), (1,)), ((), ())), preferred_element_type=F32)


def dot_left_t(a, b):
    return lax.dot_general(a, b, (((0,), (0,)), ((), ())), preferred_element_type=F32)


def row_sum(parts):
    total = parts[0]
    for part in parts[1:]:
        total = total + part
    return jnp.sum(total, axis=-1, keepdims=True)


def tile_iota(axis):
    return lax.broadcasted_iota(jnp.int32, (BLOCK, BLOCK), axis)


def norm_tokens(tokens_ref, normed_ref, normed_b_ref, inverse_ref):
    def body(b, carry):
        rows = pl.ds(pl.multiple_of(b * BLOCK, BLOCK), BLOCK)
        x = tokens_ref[rows, :].astype(F32)
        centered = x - jnp.mean(x, axis=-1, keepdims=True)
        inverse = lax.rsqrt(jnp.mean(centered * centered, axis=-1, keepdims=True) + EPSILON)
        normed = centered * inverse
        normed_ref[rows, :] = normed
        normed_b_ref[rows, :] = normed.astype(BF16)
        inverse_ref[rows, :] = jnp.broadcast_to(inverse, (BLOCK, BLOCK))
        return carry

    lax.fori_loop(0, BLOCKS, body, 0)


def project(head, normed_b_ref, weight_ref, acts_ref, slope_ref):
    for c in range(2):
        lanes = pl.ds(c * 256, 256)
        half = dot(normed_b_ref[...], weight_ref[head, :, lanes]) * 0.5
        u = 1.0 + jnp.tanh(half)
        act = half * u
        slope_ref[head, :, lanes] = 0.5 * (u + act * (2.0 - u))
        acts_ref[head, :, lanes] = act.astype(BF16)


def take_upstream(own_ref, received_ref, slot_ref, length_ref, first_ref, upstream_ref):
    def body(b, carry):
        rows = pl.ds(pl.multiple_of(b * BLOCK, BLOCK), BLOCK)
        slot = jnp.full((BLOCK, D), lax.rem(slot_ref[b], SLOTS), jnp.int32)
        value = own_ref[0:BLOCK, :].astype(F32)
        for at in range(1, SLOTS):
            ref, row_at = (own_ref, at * BLOCK) if at < BLOCKS else (received_ref, (at - BLOCKS) * BLOCK)
            value = jnp.where(slot == at, ref[row_at : row_at + BLOCK, :].astype(F32), value)
        limit = length_ref[b] - (b - first_ref[b]) * BLOCK
        row = lax.broadcasted_iota(jnp.int32, (BLOCK, D), 0)
        value = jnp.where(row < limit, value, 0.0)
        upstream_ref[rows, :] = value.astype(BF16)
        return carry

    lax.fori_loop(0, BLOCKS, body, 0)


def mix_back(upstream_ref, out_weight_ref, d_mixed_ref):
    for c in range(2):
        part = dot_right_t(upstream_ref[...], out_weight_ref[c * 256 : (c + 1) * 256, :])
        for k in range(2):
            d_mixed_ref[2 * c + k] = part[:, k * 128 : (k + 1) * 128]


def bucket_bounds(apart):
    distance = tile_iota(0) - tile_iota(1) + apart * BLOCK
    return distance, [(bucket, 0 if bucket == 0 else 2 ** (bucket - 1)) for bucket in BUCKETS_AT[apart]]


def bias_tiles(table_ref, head):
    tiles = []
    for apart in range(BLOCKS):
        distance, bounds = bucket_bounds(apart)
        tile = jnp.full((BLOCK, BLOCK), table_ref[head, bounds[0][0]] * 0.5, F32)
        for bucket, least in bounds[1:]:
            tile = jnp.where(distance >= least, table_ref[head, bucket] * 0.5, tile)
        tiles.append(tile)
    return tiles


def attend(head, acts_ref, table_ref, length_ref, first_ref, weights_ref, factor_ref, attended_ref):
    bias = bias_tiles(table_ref, head)
    row = tile_iota(0)
    causal_row = jnp.where(tile_iota(1) <= row, row, ROWS)
    for i in range(BLOCKS):
        rows = pl.ds(i * BLOCK, BLOCK)
        upto = (i + 1) * BLOCK
        scores = dot_right_t(acts_ref[head, rows, QUERY], acts_ref[head, 0:upto, KEY])
        for j in range(i + 1):
            lanes = pl.ds(j * BLOCK, BLOCK)
            limit = jnp.where(
                first_ref[i] == first_ref[j], length_ref[i] - (i - first_ref[i]) * BLOCK, 0
            )
            half = scores[:, j * BLOCK : (j + 1) * BLOCK] * (0.5 * SCALE) + bias[i - j]
            kept = (causal_row if i == j else row) < limit
            u = jnp.where(kept, 1.0 + jnp.tanh(half), 0.0)
            weight = half * u
            factor_ref[head, rows, lanes] = 0.5 * (u + weight * (2.0 - u))
            weights_ref[head, rows, lanes] = weight.astype(BF16)
        attended_ref[head, rows, :] = dot(
            weights_ref[head, rows, 0:upto], acts_ref[head, 0:upto, VALUE]
        )


def mix(acts_ref, attended_ref, d_mixed_ref, slope_ref, mixed_ref, d_attended_ref, d_proj_ref):
    def body(b, carry):
        rows = pl.ds(pl.multiple_of(b * BLOCK, BLOCK), BLOCK)
        heads = range(HEADS)
        att = [attended_ref[h, rows, :] for h in heads]
        mean = row_sum(att) * (1.0 / D)
        centered = [a - mean for a in att]
        inverse = lax.rsqrt(row_sum([c * c for c in centered]) * (1.0 / D) + EPSILON)
        normed = [c * inverse for c in centered]
        gate = [acts_ref[h, rows, GATE].astype(F32) for h in heads]
        d_mixed = [d_mixed_ref[h, rows, :] for h in heads]
        g = [d_mixed[h] * gate[h] for h in heads]
        g_mean = row_sum(g) * (1.0 / D)
        g_dot = row_sum([g[h] * normed[h] for h in heads]) * (1.0 / D)
        for h in heads:
            mixed_ref[rows, pl.ds(h * 128, 128)] = (normed[h] * gate[h]).astype(BF16)
            d_attended_ref[h, rows, :] = (inverse * (g[h] - g_mean - normed[h] * g_dot)).astype(BF16)
            d_proj_ref[h, rows, GATE] = (d_mixed[h] * normed[h] * slope_ref[h, rows, GATE]).astype(BF16)
        return carry

    lax.fori_loop(0, BLOCKS, body, 0)


def attend_back(
    head, acts_ref, weights_ref, factor_ref, d_attended_ref, slope_ref, d_logits_ref, d_proj_ref, bias_ref
):
    sums = [None] * BLOCKS
    for i in range(BLOCKS):
        rows = pl.ds(i * BLOCK, BLOCK)
        upto = (i + 1) * BLOCK
        d_weights = dot_right_t(d_attended_ref[head, rows, :], acts_ref[head, 0:upto, VALUE])
        for j in range(i + 1):
            lanes = pl.ds(j * BLOCK, BLOCK)
            d_logits = d_weights[:, j * BLOCK : (j + 1) * BLOCK] * factor_ref[head, rows, lanes]
            sums[i - j] = d_logits if sums[i - j] is None else sums[i - j] + d_logits
            d_logits_ref[rows, lanes] = d_logits.astype(BF16)
        d_query = dot(d_logits_ref[rows, 0:upto], acts_ref[head, 0:upto, KEY])
        d_proj_ref[head, rows, QUERY] = (d_query * SCALE * slope_ref[head, rows, QUERY]).astype(BF16)
    for j in range(BLOCKS):
        rows = pl.ds(j * BLOCK, BLOCK)
        below = pl.ds(j * BLOCK, ROWS - j * BLOCK)
        d_value = dot_left_t(weights_ref[head, below, rows], d_attended_ref[head, below, :])
        d_proj_ref[head, rows, VALUE] = (d_value * slope_ref[head, rows, VALUE]).astype(BF16)
        d_key = dot_left_t(d_logits_ref[below, rows], acts_ref[head, below, QUERY])
        d_proj_ref[head, rows, KEY] = (d_key * SCALE * slope_ref[head, rows, KEY]).astype(BF16)
    totals = [None] * BUCKETS
    for apart in range(BLOCKS):
        distance, bounds = bucket_bounds(apart)
        for at, (bucket, least) in enumerate(bounds):
            value = sums[apart]
            if at > 0:
                value = jnp.where(distance >= least, value, 0.0)
            if at + 1 < len(bounds):
                value = jnp.where(distance < bounds[at + 1][1], value, 0.0)
            value = jnp.sum(value, axis=0, keepdims=True)
            totals[bucket] = value if totals[bucket] is None else totals[bucket] + value
    lane = lax.broadcasted_iota(jnp.int32, (1, 128), 1)
    packed = jnp.zeros((1, 128), F32)
    for bucket in range(BUCKETS):
        packed = jnp.where(lane == bucket, jnp.sum(totals[bucket], axis=1, keepdims=True), packed)
    bias_ref[pl.ds(head, 1), :] = packed


def token_grads(part, d_proj_ref, weight_ref, normed_ref, inverse_ref, upstream_ref, token_grad_ref):
    rows = pl.ds(part * 256, 256)
    d_normed = dot_right_t(d_proj_ref[0, rows, :], weight_ref[0])
    for h in range(1, HEADS):
        d_normed = d_normed + dot_right_t(d_proj_ref[h, rows, :], weight_ref[h])
    normed = normed_ref[rows, :]
    inverse = inverse_ref[rows, 0:1]
    mean = jnp.mean(d_normed, axis=-1, keepdims=True)
    along = jnp.mean(d_normed * normed, axis=-1, keepdims=True)
    back = inverse * (d_normed - mean - normed * along)
    token_grad_ref[rows, :] = (upstream_ref[rows, :].astype(F32) + back).astype(BF16)


def place():
    dp = lax.axis_index("dp")
    return lax.axis_index("rep"), lax.div(dp, 2 * NZ), lax.rem(lax.div(dp, 2), NZ), lax.rem(dp, 2)


def device(x, y, z, core):
    return ((y * NZ + z) * 2 + core, x)


def layer_kernel(
    tokens_hbm, cotangent_hbm, weight_hbm, out_weight_hbm, table_hbm, length_hbm, first_hbm, slot_hbm,
    token_grad_ref, proj_grad_ref, out_grad_ref, bias_grad_ref,
    tokens_ref, own_ref, received_ref, weight_ref, out_weight_ref, table_ref, length_ref, first_ref, slot_ref,
    normed_ref, normed_b_ref, inverse_ref, acts_ref, slope_ref, upstream_ref, d_mixed_ref, weights_ref,
    factor_ref, attended_ref, mixed_ref, d_attended_ref, d_logits_ref, d_proj_ref,
    term, core_in, x_out, x_in, x_sum, y_in, y_sum, z_in, column_sum, column_in,
    out_y_in, out_z_all, out_mine, out_x_all, out_core_in,
    bias_core, bias_x, bias_y, bias_z,
    load_sem, cotangent_sem, core_sem, x_sem, y_send, y_recv, z_sem, column_sem,
    out_y_sem, out_z_sem, out_y_back_sem, out_x_back_sem, out_core_back_sem,
    bias_core_sem, bias_x_sem, bias_y_sem, bias_z_sem,
):
    x, y, z, core = place()
    other = 1 - core
    dp = lax.axis_index("dp")
    n_dp = 2 * NY * NZ

    def x_peer(k):
        return lax.rem(x + k, NX)

    def y_peer(k):
        return lax.rem(y + k, NY)

    def z_peer(k):
        return lax.rem(z + k, NZ)

    def remote(src, dst, send, recv, target):
        return pltpu.make_async_remote_copy(
            src_ref=src, dst_ref=dst, send_sem=send, recv_sem=recv, device_id=target,
            device_id_type=pl.DeviceIdType.MESH,
        )

    loads = [
        pltpu.make_async_copy(tokens_hbm, tokens_ref, load_sem.at[0]),
        pltpu.make_async_copy(table_hbm, table_ref, load_sem.at[1]),
        pltpu.make_async_copy(length_hbm, length_ref, load_sem.at[2]),
        pltpu.make_async_copy(first_hbm, first_ref, load_sem.at[3]),
        pltpu.make_async_copy(slot_hbm, slot_ref, load_sem.at[4]),
        pltpu.make_async_copy(cotangent_hbm.at[pl.ds(0, ROWS)], own_ref, load_sem.at[5]),
        pltpu.make_async_copy(out_weight_hbm, out_weight_ref, load_sem.at[6]),
    ]
    weight_loads = [
        pltpu.make_async_copy(
            weight_hbm.at[:, pl.ds(g * D + h * 128, 128)],
            weight_ref.at[h, :, pl.ds(g * 128, 128)],
            load_sem.at[7 + h * 4 + g],
        )
        for h in range(HEADS)
        for g in range(4)
    ]
    for load in loads[:1] + weight_loads + loads[1:]:
        load.start()

    barrier = pltpu.get_barrier_semaphore()
    greeted = [device(x, y, z, other)]
    greeted += [device(x_peer(k), y, z, core) for k in range(1, NX)]
    greeted += [device(x, y_peer(k), z, core) for k in range(1, NY)]
    greeted += [device(x, y, z_peer(k), core) for k in range(1, NZ)]
    greeted += [(lax.rem(dp + n_dp + 2 * core - 1, n_dp), x)]
    for target in greeted:
        pl.semaphore_signal(barrier, inc=1, device_id=target, device_id_type=pl.DeviceIdType.MESH)

    loads[0].wait()
    norm_tokens(tokens_ref, normed_ref, normed_b_ref, inverse_ref)

    pl.semaphore_wait(barrier, len(greeted))
    cotangent_copy = remote(
        cotangent_hbm.at[pl.ds(ROWS, 2 * BLOCK)], received_ref, cotangent_sem.at[0], cotangent_sem.at[1],
        (lax.rem(dp + n_dp - 1, n_dp), x),
    )
    cotangent_copy.start()

    for load in weight_loads + loads[1:]:
        load.wait()

    def forward(head, carry):
        project(head, normed_b_ref, weight_ref, acts_ref, slope_ref)
        attend(head, acts_ref, table_ref, length_ref, first_ref, weights_ref, factor_ref, attended_ref)
        return carry

    lax.fori_loop(0, HEADS, forward, 0)

    cotangent_copy.wait_recv()
    take_upstream(own_ref, received_ref, slot_ref, length_ref, first_ref, upstream_ref)
    mix_back(upstream_ref, out_weight_ref, d_mixed_ref)
    mix(acts_ref, attended_ref, d_mixed_ref, slope_ref, mixed_ref, d_attended_ref, d_proj_ref)

    def put_term(s, value):
        term[s] = value.astype(BF16).reshape(4, 4, 2, 16, D)

    def core_copy(s):
        return remote(
            term.at[s, :, :, other], core_in.at[s], core_sem.at[0, s], core_sem.at[1, s],
            device(x, y, z, other),
        )

    def x_copy(s, k):
        return remote(
            x_out.at[s, x_peer(k)], x_in.at[s, k - 1], x_sem.at[0, s, k - 1], x_sem.at[1, s, k - 1],
            device(x_peer(k), y, z, core),
        )

    def after_core(s):
        core_copy(s).wait_recv()

        def body(g, carry):
            for zz in range(4):
                both = term[s, g, zz, core].astype(F32) + core_in[s, g, zz].astype(F32)
                both = both.astype(BF16)
                for k in range(NX):
                    x_out[s, k, g, zz] = both[:, k * 128 : (k + 1) * 128]
            return carry

        lax.fori_loop(0, 4, body, 0)
        for k in (2, 1, 3):
            x_copy(s, k).start()

    def after_x(s):
        for k in range(1, NX):
            x_copy(s, k).wait_recv()

        def body(g, carry):
            total = x_out[s, x, g].astype(F32)
            for k in range(NX - 1):
                total = total + x_in[s, k, g].astype(F32)
            x_sum[s, g] = total.astype(BF16)
            return carry

        lax.fori_loop(0, 4, body, 0)

    def y_copy(h, g):
        to_y = 2 * g + lax.div(h, 2)
        slot = lax.rem(lax.rem(y - to_y + NY - 1, NY), NY - 1)
        return to_y != y, remote(
            x_sum.at[1 + h, g],
            y_in.at[lax.rem(h, 2), slot],
            y_send.at[h, g],
            y_recv.at[lax.rem(h, 2), slot],
            device(x, to_y, z, core),
        )

    def y_start(h):
        for g in range(4):
            away, copy = y_copy(h, g)
            pl.when(away)(copy.start)

    def after_y(h):
        @pl.when(lax.rem(y, 2) == lax.div(h, 2))
        def _():
            half = lax.rem(h, 2)
            for k in range(NY - 1):
                remote(
                    x_sum.at[1 + h, 0], y_in.at[half, k], y_send.at[h, 0], y_recv.at[half, k],
                    device(x, y_peer(1), z, core),
                ).wait_recv()
            total = x_sum[1 + h, lax.div(y, 2)].astype(F32)
            for k in range(NY - 1):
                total = total + y_in[half, k].astype(F32)
            y_sum[half] = total.astype(BF16)

    def out_chunk(ref, at_y, *lead):
        return ref.at[(*lead, lax.div(at_y, 2), pl.ds(lax.rem(at_y, 2) * 2, 2))]

    def out_y_copy(k):
        return remote(
            out_chunk(x_sum, y_peer(k), 0), out_y_in.at[k - 1], out_y_sem.at[0, k - 1],
            out_y_sem.at[1, k - 1], device(x, y_peer(k), z, core),
        )

    def out_z_copy(k):
        return remote(
            out_z_all.at[z], out_z_all.at[z], out_z_sem.at[0, k - 1], out_z_sem.at[1, k - 1],
            device(x, y, z_peer(k), core),
        )

    def out_y_back_copy(k):
        return remote(
            out_chunk(out_mine, y), out_chunk(out_mine, y), out_y_back_sem.at[0, k - 1],
            out_y_back_sem.at[1, k - 1], device(x, y_peer(k), z, core),
        )

    def out_x_back_copy(k):
        return remote(
            out_mine, out_x_all.at[x], out_x_back_sem.at[0, k - 1], out_x_back_sem.at[1, k - 1],
            device(x_peer(k), y, z, core),
        )

    out_core_back_copy = remote(
        out_x_all, out_core_in, out_core_back_sem.at[0], out_core_back_sem.at[1], device(x, y, z, other)
    )

    def out_y_start():
        for k in range(1, NY):
            out_y_copy(k).start()

    def out_after_y():
        for k in range(1, NY):
            out_y_copy(k).wait_recv()
        total = out_chunk(x_sum, y, 0)[...].astype(F32)
        for k in range(NY - 1):
            total = total + out_y_in[k].astype(F32)
        out_z_all[z] = total.astype(BF16)
        for k in range(1, NZ):
            out_z_copy(k).start()

    def out_after_z():
        for k in range(1, NZ):
            out_z_copy(k).wait_recv()
        total = out_z_all[0].astype(F32)
        for k in range(1, NZ):
            total = total + out_z_all[k].astype(F32)
        out_chunk(out_mine, y)[...] = total.astype(BF16)
        for k in range(1, NY):
            out_y_back_copy(k).start()

    def out_after_y_back():
        for k in range(1, NY):
            out_y_back_copy(k).wait_recv()
        out_x_all[x] = out_mine[...]
        for k in range(1, NX):
            out_x_back_copy(k).start()

    def out_after_x_back():
        for k in range(1, NX):
            out_x_back_copy(k).wait_recv()
        out_core_back_copy.start()

    def out_finish():
        out_core_back_copy.wait_recv()
        for from_core, gathered in ((core, out_x_all), (other, out_core_in)):
            for g in range(4):
                for zz in range(4):
                    at = pl.multiple_of(g * 128 + zz * 32 + from_core * 16, 16)
                    for k in range(NX):
                        out_grad_ref[pl.ds(at, 16), k * 128 : (k + 1) * 128] = gathered[k, g, zz]

    bias_steps = (
        (bias_core, bias_core_sem, core, 2, lambda k: device(x, y, z, other)),
        (bias_x, bias_x_sem, x, NX, lambda k: device(x_peer(k), y, z, core)),
        (bias_y, bias_y_sem, y, NY, lambda k: device(x, y_peer(k), z, core)),
        (bias_z, bias_z_sem, z, NZ, lambda k: device(x, y, z_peer(k), core)),
    )

    def bias_copies(step):
        buffer, sems, at, count, peer = bias_steps[step]
        return [
            remote(buffer.at[at], buffer.at[at], sems.at[0, k - 1], sems.at[1, k - 1], peer(k))
            for k in range(1, count)
        ]

    def bias_start(step, value):
        bias_steps[step][0][bias_steps[step][2]] = value
        for copy in bias_copies(step):
            copy.start()

    def bias_finish(step):
        for copy in bias_copies(step):
            copy.wait_recv()
        buffer, count = bias_steps[step][0], bias_steps[step][3]
        total = buffer[0]
        for k in range(1, count):
            total = total + buffer[k]
        return total

    put_term(0, dot_left_t(mixed_ref[...], upstream_ref[...]))
    core_copy(0).start()
    bias_grad_ref[...] = jnp.zeros_like(bias_grad_ref)

    def backward(head, carry):
        attend_back(
            head, acts_ref, weights_ref, factor_ref, d_attended_ref, slope_ref, d_logits_ref, d_proj_ref,
            bias_grad_ref,
        )
        after_core(head)

        @pl.when(head >= 1)
        def _():
            after_x(head - 1)

        pl.when(head == 1)(out_y_start)

        @pl.when(head >= 2)
        def _():
            y_start(head - 2)

        pl.when(head == 2)(out_after_y)

        @pl.when(head == 3)
        def _():
            after_y(0)
            out_after_z()

        put_term(1 + head, dot_left_t(d_proj_ref[head], normed_b_ref[...]))
        core_copy(1 + head).start()
        return carry

    lax.fori_loop(0, HEADS, backward, 0)

    bias_start(0, bias_grad_ref[...])
    token_grads(0, d_proj_ref, weight_ref, normed_ref, inverse_ref, upstream_ref, token_grad_ref)
    after_core(4)
    bias_start(1, bias_finish(0))
    after_x(3)
    y_start(2)
    after_y(1)
    out_after_y_back()
    token_grads(1, d_proj_ref, weight_ref, normed_ref, inverse_ref, upstream_ref, token_grad_ref)
    after_x(4)
    y_start(3)
    bias_start(2, bias_finish(1))
    after_y(2)
    out_after_x_back()
    after_y(3)

    def z_copy(k):
        to_z = z_peer(k)
        return remote(
            y_sum.at[lax.div(to_z, 4), lax.rem(to_z, 4)], z_in.at[k - 1], z_sem.at[0, k - 1],
            z_sem.at[1, k - 1], device(x, y, to_z, core),
        )

    for k in range(1, NZ):
        z_copy(k).start()
    bias_start(3, bias_finish(2))
    out_finish()
    for k in range(1, NZ):
        z_copy(k).wait_recv()
    total = y_sum[lax.div(z, 4), lax.rem(z, 4)].astype(F32)
    for k in range(NZ - 1):
        total = total + z_in[k].astype(F32)
    column_sum[...] = total

    def column_copy(k):
        return remote(
            column_sum, column_in.at[k - 1], column_sem.at[0, k - 1], column_sem.at[1, k - 1],
            device(x_peer(k), y, z, core),
        )

    for k in range(1, NX):
        column_copy(k).start()
    bias_grad_ref[...] = bias_finish(3)

    for k in range(1, NX):
        column_copy(k).wait_recv()
    for k in range(NX):
        part = column_sum[...] if k == 0 else column_in[k - 1]
        mine = part[0:4]
        for at in range(1, NX):
            mine = jnp.where(jnp.full((4, 128), x, jnp.int32) == at, part[4 * at : 4 * at + 4], mine)
        from_x = lax.rem(x + NX - k, NX)
        proj_grad_ref[:, pl.ds(pl.multiple_of(from_x * 128, 128), 128)] = mine

    cotangent_copy.wait_send()
    for s in range(SETS):
        core_copy(s).wait_send()
        for k in range(1, NX):
            x_copy(s, k).wait_send()
    for h in range(HEADS):
        for g in range(4):
            away, copy = y_copy(h, g)
            pl.when(away)(copy.wait_send)
    for k in range(1, NY):
        out_y_copy(k).wait_send()
        out_y_back_copy(k).wait_send()
    for k in range(1, NZ):
        out_z_copy(k).wait_send()
        z_copy(k).wait_send()
    for k in range(1, NX):
        out_x_back_copy(k).wait_send()
        column_copy(k).wait_send()
    out_core_back_copy.wait_send()
    for step in range(4):
        for copy in bias_copies(step):
            copy.wait_send()


DMA = pltpu.SemaphoreType.DMA
ARGUMENT_SCRATCH = [
    pltpu.VMEM((ROWS, D), BF16),
    pltpu.VMEM((ROWS, D), BF16),
    pltpu.VMEM((2 * BLOCK, D), BF16),
    pltpu.VMEM((HEADS, D, D), BF16),
    pltpu.VMEM((D, D), BF16),
    pltpu.SMEM((HEADS, BUCKETS), F32),
    pltpu.SMEM((BLOCKS,), jnp.int32),
    pltpu.SMEM((BLOCKS,), jnp.int32),
    pltpu.SMEM((BLOCKS,), jnp.int32),
]
LAYER_SCRATCH = [
    pltpu.VMEM((ROWS, D), F32),
    pltpu.VMEM((ROWS, D), BF16),
    pltpu.VMEM((ROWS, BLOCK), F32),
    pltpu.VMEM((HEADS, ROWS, D), BF16),
    pltpu.VMEM((HEADS, ROWS, D), F32),
    pltpu.VMEM((ROWS, D), BF16),
    pltpu.VMEM((HEADS, ROWS, 128), F32),
    pltpu.VMEM((HEADS, ROWS, ROWS), BF16),
    pltpu.VMEM((HEADS, ROWS, ROWS), F32),
    pltpu.VMEM((HEADS, ROWS, 128), F32),
    pltpu.VMEM((ROWS, D), BF16),
    pltpu.VMEM((HEADS, ROWS, 128), BF16),
    pltpu.VMEM((ROWS, ROWS), BF16),
    pltpu.VMEM((HEADS, ROWS, D), BF16),
]
SUM_SCRATCH = [
    pltpu.VMEM((SETS, 4, 4, 2, 16, D), BF16),
    pltpu.VMEM((SETS, 4, 4, 16, D), BF16),
    pltpu.VMEM((SETS, NX, 4, 4, 16, 128), BF16),
    pltpu.VMEM((SETS, NX - 1, 4, 4, 16, 128), BF16),
    pltpu.VMEM((SETS, 4, 4, 16, 128), BF16),
    pltpu.VMEM((2, NY - 1, 4, 16, 128), BF16),
    pltpu.VMEM((2, 4, 16, 128), BF16),
    pltpu.VMEM((NZ - 1, 16, 128), BF16),
    pltpu.VMEM((16, 128), F32),
    pltpu.VMEM((NX - 1, 16, 128), F32),
    pltpu.VMEM((NY - 1, 2, 16, 128), BF16),
    pltpu.VMEM((NZ, 2, 16, 128), BF16),
    pltpu.VMEM((4, 4, 16, 128), BF16),
    pltpu.VMEM((NX, 4, 4, 16, 128), BF16),
    pltpu.VMEM((NX, 4, 4, 16, 128), BF16),
    pltpu.VMEM((2, 8, 128), F32),
    pltpu.VMEM((NX, 8, 128), F32),
    pltpu.VMEM((NY, 8, 128), F32),
    pltpu.VMEM((NZ, 8, 128), F32),
]
SEMAPHORES = [
    DMA((23,)),
    DMA((2,)),
    DMA((2, SETS)),
    DMA((2, SETS, NX - 1)),
    DMA((HEADS, 4)),
    DMA((2, NY - 1)),
    DMA((2, NZ - 1)),
    DMA((2, NX - 1)),
    DMA((2, NY - 1)),
    DMA((2, NZ - 1)),
    DMA((2, NY - 1)),
    DMA((2, NX - 1)),
    DMA((2,)),
    DMA((2, 1)),
    DMA((2, NX - 1)),
    DMA((2, NY - 1)),
    DMA((2, NZ - 1)),
]


def shards(tokens, cotangent, weight, out_weight, table, length, first, slot):
    vmem = pl.BlockSpec(memory_space=pltpu.VMEM)
    token_grad, proj_grad, out_grad, bias_grad = pl.pallas_call(
        layer_kernel,
        out_shape=(
            jax.ShapeDtypeStruct((ROWS, D), BF16),
            jax.ShapeDtypeStruct((4, D), F32),
            jax.ShapeDtypeStruct((D, D), BF16),
            jax.ShapeDtypeStruct((8, 128), F32),
        ),
        in_specs=[pl.BlockSpec(memory_space=pl.ANY)] * 8,
        out_specs=(vmem,) * 4,
        scratch_shapes=ARGUMENT_SCRATCH + LAYER_SCRATCH + SUM_SCRATCH + SEMAPHORES,
        compiler_params=pltpu.CompilerParams(
            vmem_limit_bytes=52 * 2**20, collective_id=0, has_side_effects=True
        ),
        name="layer_grads",
    )(tokens, cotangent, weight, out_weight, table, length, first, slot)
    return token_grad, proj_grad.T, out_grad.astype(F32), bias_grad[:HEADS, :BUCKETS]


def solution(mesh):
    split = P(("dp", "rep"))
    return jax.shard_map(
        shards,
        mesh=mesh,
        in_specs=(split, split, P(), P(), P(), split, split, split),
        out_specs=(split, P(None, ("dp", "rep")), P(), P()),
        check_vma=False,
    )
```

time: 350 us -> 68.8 us (0.20)
  waiting for transfers between devices: 185 us -> 0 us
  blocking collectives: 109 us -> 0 us
  Pallas kernels: 21.9 us -> 60.8 us
  between operations: 14.1 us -> 0.66 us
  starting transfers between devices: 8.82 us -> 0 us
  local copies, waits for them, and re-layouts: 9.86 us -> 5.65 us
    unnamed x2 -> x0, waiting for transfers between devices: 184 us -> none
    psum x1 -> x0, blocking collectives: 109 us -> none  [shards(): out_grad, bias_grad = lax.psum((out_term, bias_term), ('dp', 'rep'))]
    pallas_call x1, Pallas kernels: 21.9 us -> 60.8 us  [shards(): pl.pallas_call(layer_kernel, out_shape=(jax.ShapeDtypeStruct((ROWS, D), B...]
    ppermute x1 -> x0, starting transfers between devices: 8.79 us -> none  [shards(): lax.ppermute(cotangent[ROWS:], 'dp', [(source, (source - 1) % count) for...]
  transfers between devices with their start and end apart: 2 -> 0, of which waited for: 2 -> 0; matrix products, arithmetic and copies ran while one was open for 0% -> 0% of each run, Pallas kernels for 0% -> 0%
where the time goes in v2:
time: 68.8 us; the launch traced here: 68.2 us
  Pallas kernels  60.8 us (88%)
  local copies, waits for them, and re-layouts  5.65 us (8%)
  other arithmetic  1.1 us (2%)
    pallas_call x1, Pallas kernels, shards(): pl.pallas_call(layer_kernel, out_shape=(jax.ShapeDtypeStruct((ROWS, D), B...  60.8 us
    unnamed x12, local copies, waits for them, and re-layouts  5.07 us

profile of v2, /device:TPU:1, one launch (start us, length us, event | category | flops | bytes accessed | tf_op | source)
XLA Modules:
  0.0 68.2 jit_solution(2742740866063821778)
XLA Ops:
  0.6 0.0 copy-start
  0.6 1.0 %copy-done = bf16[512,512]{1,0:T(8,128)(2,1)S(1)} copy-done((bf16[512,512]{1,0:T(8,128)(2,1)S(1)}, bf16[512,512]{1,0:T(8,128)(2,1)}, u32[]{:S(2)}) %copy-start) | copy-done | bytes 524312
  1.7 0.0 copy-start.1
  1.7 0.7 copy-done.1
  2.4 0.0 copy-start.2
  2.4 0.7 copy-done.2
  3.0 0.0 copy-start.3
  3.0 0.7 copy-done.3
  3.7 0.0 copy-start.4
  3.7 0.7 copy-done.4
  4.3 60.8 %layer_grads.1 = (bf16[512,512]{1,0:T(8,128)(2,1)S(1)}, f32[4,512]{1,0:T(4,128)S(1)}, bf16[512,512]{1,0:T(8,128)(2,1)S(1)}, f32[8,128]{1,0:T(8,128)S(1)}) custom-call(bf16[512,512]{1,0:T(8,128)(2,1)S(1)} %copy-done, bf16[768,512]{1,0:T(8,128)(2,1)} %cotangent_hbm.1, bf16[512,2048]{1,0:T(8,128)(2,1)} %weight_hbm.1, bf16[512,512]{1,0:T(8,128)(2,1)} %out_weight_hbm.1, ...), custom_call_target="tpu_custom_call" | custom-call | tf_op jit(solution)/shard_map/layer_grads/pallas_call | solution.py:672
  65.1 0.6 slice.3
  65.7 1.1 %convert_element_type.3 = f32[512,512]{1,0:T(8,128)} convert(bf16[512,512]{1,0:T(8,128)(2,1)S(1)} %get-tuple-element.10) | non-fusion elementwise | flops 262144 | bytes 1572864 | tf_op jit(solution)/shard_map/convert_element_type | solution.py:688
  66.8 0.8 %copy.14 = bf16[512,512]{1,0:T(8,128)(2,1)} copy(bf16[512,512]{1,0:T(8,128)(2,1)S(1)} %get-tuple-element.16) | data formatting | bytes 1048576
  67.6 0.6 copy.15
Async XLA Ops:
  0.6 1.0 %copy-start = (bf16[512,512]{1,0:T(8,128)(2,1)S(1)}, bf16[512,512]{1,0:T(8,128)(2,1)}, u32[]{:S(2)}) copy-start(bf16[512,512]{1,0:T(8,128)(2,1)} %tokens_hbm.1) | copy-start | bytes 1572868
  1.7 0.7 copy-start.1
  2.4 0.7 copy-start.2
  3.0 0.7 copy-start.3
  3.7 0.7 copy-start.4

commit v3 on v2

--- a/solution.py
+++ b/solution.py
@@ -12,7 +12,7 @@
 SLOTS = 6
 BUCKETS = 10
 NX, NY, NZ = 4, 8, 8
-SETS = HEADS + 1
+SETS = HEADS + 2
 D = 512
 ROWS = BLOCKS * BLOCK
 EPSILON = 1e-06
@@ -226,10 +226,10 @@
     tokens_ref, own_ref, received_ref, weight_ref, out_weight_ref, table_ref, length_ref, first_ref, slot_ref,
     normed_ref, normed_b_ref, inverse_ref, acts_ref, slope_ref, upstream_ref, d_mixed_ref, weights_ref,
     factor_ref, attended_ref, mixed_ref, d_attended_ref, d_logits_ref, d_proj_ref,
-    term, core_in, x_out, x_in, x_sum, y_in, y_sum, z_in, column_sum, column_in,
+    term, core_in, x_out, x_in, x_sum, y_in, y_sum, z_in,
     out_y_in, out_z_all, out_mine, out_x_all, out_core_in,
     bias_core, bias_x, bias_y, bias_z,
-    load_sem, cotangent_sem, core_sem, x_sem, y_send, y_recv, z_sem, column_sem,
+    load_sem, cotangent_sem, core_sem, x_sem, y_send, y_recv, z_sem,
     out_y_sem, out_z_sem, out_y_back_sem, out_x_back_sem, out_core_back_sem,
     bias_core_sem, bias_x_sem, bias_y_sem, bias_z_sem,
 ):
@@ -262,15 +262,15 @@
         pltpu.make_async_copy(cotangent_hbm.at[pl.ds(0, ROWS)], own_ref, load_sem.at[5]),
         pltpu.make_async_copy(out_weight_hbm, out_weight_ref, load_sem.at[6]),
     ]
-    weight_loads = [
-        pltpu.make_async_copy(
-            weight_hbm.at[:, pl.ds(g * D + h * 128, 128)],
+
+    def weight_load(h, g):
+        return pltpu.make_async_copy(
+            weight_hbm.at[:, pl.ds(pl.multiple_of(g * D + h * 128, 128), 128)],
             weight_ref.at[h, :, pl.ds(g * 128, 128)],
             load_sem.at[7 + h * 4 + g],
         )
-        for h in range(HEADS)
-        for g in range(4)
-    ]
+
+    weight_loads = [weight_load(h, g) for h in range(HEADS) for g in range(4)]
     for load in loads[:1] + weight_loads + loads[1:]:
         load.start()
 
@@ -293,35 +293,59 @@
     )
     cotangent_copy.start()
 
-    for load in weight_loads + loads[1:]:
+    for load in loads[1:5]:
         load.wait()
 
     def forward(head, carry):
+        for g in range(4):
+            weight_load(head, g).wait()
         project(head, normed_b_ref, weight_ref, acts_ref, slope_ref)
         attend(head, acts_ref, table_ref, length_ref, first_ref, weights_ref, factor_ref, attended_ref)
         return carry
 
     lax.fori_loop(0, HEADS, forward, 0)
 
+    for load in loads[5:]:
+        load.wait()
     cotangent_copy.wait_recv()
     take_upstream(own_ref, received_ref, slot_ref, length_ref, first_ref, upstream_ref)
     mix_back(upstream_ref, out_weight_ref, d_mixed_ref)
     mix(acts_ref, attended_ref, d_mixed_ref, slope_ref, mixed_ref, d_attended_ref, d_proj_ref)
 
     def put_term(s, value):
-        term[s] = value.astype(BF16).reshape(4, 4, 2, 16, D)
+        units = value.shape[0] // 128
+        term[s, 0:units] = value.astype(BF16).reshape(units, 4, 2, 16, D)
+
+    def units_of(s):
+        return pl.ds(0, 4 if s < 2 else 3)
 
     def core_copy(s):
         return remote(
-            term.at[s, :, :, other], core_in.at[s], core_sem.at[0, s], core_sem.at[1, s],
+            term.at[s, units_of(s), :, other], core_in.at[s, units_of(s)], core_sem.at[0, s], core_sem.at[1, s],
             device(x, y, z, other),
         )
 
     def x_copy(s, k):
         return remote(
-            x_out.at[s, x_peer(k)], x_in.at[s, k - 1], x_sem.at[0, s, k - 1], x_sem.at[1, s, k - 1],
+            x_out.at[s, x_peer(k), units_of(s)], x_in.at[s, k - 1, units_of(s)], x_sem.at[0, s, k - 1], x_sem.at[1, s, k - 1],
             device(x_peer(k), y, z, core),
         )
+
+    def by_lanes(both):
+        return [both[:, k * 128 : (k + 1) * 128] for k in range(NX)]
+
+    def by_columns(both):
+        upper = lax.broadcasted_iota(jnp.int32, (8, 128), 0) < 4
+        parts = []
+        for k in range(NX):
+            rows = both[(k // 2) * 8 : (k // 2) * 8 + 8]
+            quarters = [rows[:, q * 128 : (q + 1) * 128] for q in range(4)]
+            if k % 2 == 0:
+                pairs = [jnp.where(upper, quarters[q], pltpu.roll(quarters[q + 1], 4, 0)) for q in (0, 2)]
+            else:
+                pairs = [jnp.where(upper, pltpu.roll(quarters[q], 4, 0), quarters[q + 1]) for q in (0, 2)]
+            parts.append(jnp.concatenate(pairs, axis=0))
+        return parts
 
     def after_core(s):
         core_copy(s).wait_recv()
@@ -329,57 +353,60 @@
         def body(g, carry):
             for zz in range(4):
                 both = term[s, g, zz, core].astype(F32) + core_in[s, g, zz].astype(F32)
-                both = both.astype(BF16)
-                for k in range(NX):
-                    x_out[s, k, g, zz] = both[:, k * 128 : (k + 1) * 128]
+                for k, part in enumerate(by_lanes(both) if s == 0 else by_columns(both)):
+                    x_out[s, k, g, zz] = part.astype(BF16)
             return carry
 
-        lax.fori_loop(0, 4, body, 0)
+        lax.fori_loop(0, 4 if s < 2 else 3, body, 0)
         for k in (2, 1, 3):
             x_copy(s, k).start()
 
     def after_x(s):
         for k in range(1, NX):
             x_copy(s, k).wait_recv()
-
-        def body(g, carry):
+        for g in range(4 if s < 2 else 3):
             total = x_out[s, x, g].astype(F32)
             for k in range(NX - 1):
                 total = total + x_in[s, k, g].astype(F32)
             x_sum[s, g] = total.astype(BF16)
-            return carry
-
-        lax.fori_loop(0, 4, body, 0)
-
-    def y_copy(h, g):
-        to_y = 2 * g + lax.div(h, 2)
+
+    def y_copy(g, h):
+        to_y = 2 * g + h // 2
         slot = lax.rem(lax.rem(y - to_y + NY - 1, NY), NY - 1)
         return to_y != y, remote(
-            x_sum.at[1 + h, g],
-            y_in.at[lax.rem(h, 2), slot],
-            y_send.at[h, g],
-            y_recv.at[lax.rem(h, 2), slot],
+            x_sum.at[1, h] if g == 0 else x_sum.at[2 + h, g - 1],
+            y_in.at[h % 2, slot],
+            y_send.at[g, h],
+            y_recv.at[h % 2, slot],
             device(x, to_y, z, core),
         )
 
-    def y_start(h):
-        for g in range(4):
-            away, copy = y_copy(h, g)
+    def y_start(units):
+        for g, h in units:
+            away, copy = y_copy(g, h)
             pl.when(away)(copy.start)
 
+    def add_y(half, own):
+        for k in range(NY - 1):
+            remote(
+                x_sum.at[1, 0], y_in.at[half, k], y_send.at[0, 0], y_recv.at[half, k],
+                device(x, y_peer(1), z, core),
+            ).wait_recv()
+        total = own.astype(F32)
+        for k in range(NY - 1):
+            total = total + y_in[half, k].astype(F32)
+        y_sum[half] = total.astype(BF16)
+
+    def after_y_gate():
+        @pl.when(y < 2)
+        def _():
+            for half in range(2):
+                add_y(half, x_sum[1, 2 * y + half])
+
     def after_y(h):
-        @pl.when(lax.rem(y, 2) == lax.div(h, 2))
+        @pl.when((y >= 2) & (lax.rem(y, 2) == h // 2))
         def _():
-            half = lax.rem(h, 2)
-            for k in range(NY - 1):
-                remote(
-                    x_sum.at[1 + h, 0], y_in.at[half, k], y_send.at[h, 0], y_recv.at[half, k],
-                    device(x, y_peer(1), z, core),
-                ).wait_recv()
-            total = x_sum[1 + h, lax.div(y, 2)].astype(F32)
-            for k in range(NY - 1):
-                total = total + y_in[half, k].astype(F32)
-            y_sum[half] = total.astype(BF16)
+            add_y(h % 2, x_sum[2 + h, lax.div(y, 2) - 1])
 
     def out_chunk(ref, at_y, *lead):
         return ref.at[(*lead, lax.div(at_y, 2), pl.ds(lax.rem(at_y, 2) * 2, 2))]
@@ -485,55 +512,23 @@
             total = total + buffer[k]
         return total
 
-    put_term(0, dot_left_t(mixed_ref[...], upstream_ref[...]))
-    core_copy(0).start()
-    bias_grad_ref[...] = jnp.zeros_like(bias_grad_ref)
-
-    def backward(head, carry):
+    gate_units = [(0, h) for h in range(HEADS)]
+
+    def head_units(h):
+        return [(g, h) for g in range(1, 4)]
+
+    def back(head):
         attend_back(
             head, acts_ref, weights_ref, factor_ref, d_attended_ref, slope_ref, d_logits_ref, d_proj_ref,
             bias_grad_ref,
         )
-        after_core(head)
-
-        @pl.when(head >= 1)
-        def _():
-            after_x(head - 1)
-
-        pl.when(head == 1)(out_y_start)
-
-        @pl.when(head >= 2)
-        def _():
-            y_start(head - 2)
-
-        pl.when(head == 2)(out_after_y)
-
-        @pl.when(head == 3)
-        def _():
-            after_y(0)
-            out_after_z()
-
-        put_term(1 + head, dot_left_t(d_proj_ref[head], normed_b_ref[...]))
-        core_copy(1 + head).start()
-        return carry
-
-    lax.fori_loop(0, HEADS, backward, 0)
-
-    bias_start(0, bias_grad_ref[...])
-    token_grads(0, d_proj_ref, weight_ref, normed_ref, inverse_ref, upstream_ref, token_grad_ref)
-    after_core(4)
-    bias_start(1, bias_finish(0))
-    after_x(3)
-    y_start(2)
-    after_y(1)
-    out_after_y_back()
-    token_grads(1, d_proj_ref, weight_ref, normed_ref, inverse_ref, upstream_ref, token_grad_ref)
-    after_x(4)
-    y_start(3)
-    bias_start(2, bias_finish(1))
-    after_y(2)
-    out_after_x_back()
-    after_y(3)
+
+    def send_head(head):
+        put_term(2 + head, dot_left_t(d_proj_ref[head, :, 128:D], normed_b_ref[...]))
+        core_copy(2 + head).start()
+
+    def tokens_part(part):
+        token_grads(part, d_proj_ref, weight_ref, normed_ref, inverse_ref, upstream_ref, token_grad_ref)
 
     def z_copy(k):
         to_z = z_peer(k)
@@ -542,36 +537,63 @@
             z_sem.at[1, k - 1], device(x, y, to_z, core),
         )
 
+    put_term(0, dot_left_t(mixed_ref[...], upstream_ref[...]))
+    core_copy(0).start()
+    d_gate = jnp.concatenate([d_proj_ref[h, :, GATE] for h in range(HEADS)], axis=1)
+    put_term(1, dot_left_t(d_gate, normed_b_ref[...]))
+    core_copy(1).start()
+    bias_grad_ref[...] = jnp.zeros_like(bias_grad_ref)
+    after_core(0)
+    back(0)
+    after_core(1)
+    send_head(0)
+    back(1)
+    after_core(2)
+    send_head(1)
+    back(2)
+    after_core(3)
+    after_x(0)
+    out_y_start()
+    send_head(2)
+    back(3)
+    after_core(4)
+    after_x(1)
+    y_start(gate_units)
+    send_head(3)
+    bias_start(0, bias_grad_ref[...])
+    tokens_part(0)
+    after_core(5)
+    bias_start(1, bias_finish(0))
+    tokens_part(1)
+    after_x(2)
+    y_start(head_units(0))
+    out_after_y()
+    after_x(3)
+    y_start(head_units(1))
+    after_x(4)
+    y_start(head_units(2))
+    bias_start(2, bias_finish(1))
+    after_x(5)
+    y_start(head_units(3))
+    out_after_z()
+    after_y_gate()
+    for h in range(HEADS - 1):
+        after_y(h)
+    bias_start(3, bias_finish(2))
+    out_after_y_back()
+    after_y(HEADS - 1)
     for k in range(1, NZ):
         z_copy(k).start()
-    bias_start(3, bias_finish(2))
-    out_finish()
+    out_after_x_back()
     for k in range(1, NZ):
         z_copy(k).wait_recv()
     total = y_sum[lax.div(z, 4), lax.rem(z, 4)].astype(F32)
     for k in range(NZ - 1):
         total = total + z_in[k].astype(F32)
-    column_sum[...] = total
-
-    def column_copy(k):
-        return remote(
-            column_sum, column_in.at[k - 1], column_sem.at[0, k - 1], column_sem.at[1, k - 1],
-            device(x_peer(k), y, z, core),
-        )
-
-    for k in range(1, NX):
-        column_copy(k).start()
+    for q in range(4):
+        proj_grad_ref[:, q * 128 : (q + 1) * 128] = total[4 * q : 4 * q + 4]
     bias_grad_ref[...] = bias_finish(3)
-
-    for k in range(1, NX):
-        column_copy(k).wait_recv()
-    for k in range(NX):
-        part = column_sum[...] if k == 0 else column_in[k - 1]
-        mine = part[0:4]
-        for at in range(1, NX):
-            mine = jnp.where(jnp.full((4, 128), x, jnp.int32) == at, part[4 * at : 4 * at + 4], mine)
-        from_x = lax.rem(x + NX - k, NX)
-        proj_grad_ref[:, pl.ds(pl.multiple_of(from_x * 128, 128), 128)] = mine
+    out_finish()
 
     cotangent_copy.wait_send()
     for s in range(SETS):
@@ -580,7 +602,7 @@
             x_copy(s, k).wait_send()
     for h in range(HEADS):
         for g in range(4):
-            away, copy = y_copy(h, g)
+            away, copy = y_copy(g, h)
             pl.when(away)(copy.wait_send)
     for k in range(1, NY):
         out_y_copy(k).wait_send()
@@ -590,7 +612,6 @@
         z_copy(k).wait_send()
     for k in range(1, NX):
         out_x_back_copy(k).wait_send()
-        column_copy(k).wait_send()
     out_core_back_copy.wait_send()
     for step in range(4):
         for copy in bias_copies(step):
@@ -634,8 +655,6 @@
     pltpu.VMEM((2, NY - 1, 4, 16, 128), BF16),
     pltpu.VMEM((2, 4, 16, 128), BF16),
     pltpu.VMEM((NZ - 1, 16, 128), BF16),
-    pltpu.VMEM((16, 128), F32),
-    pltpu.VMEM((NX - 1, 16, 128), F32),
     pltpu.VMEM((NY - 1, 2, 16, 128), BF16),
     pltpu.VMEM((NZ, 2, 16, 128), BF16),
     pltpu.VMEM((4, 4, 16, 128), BF16),
@@ -654,7 +673,6 @@
     DMA((HEADS, 4)),
     DMA((2, NY - 1)),
     DMA((2, NZ - 1)),
-    DMA((2, NX - 1)),
     DMA((2, NY - 1)),
     DMA((2, NZ - 1)),
     DMA((2, NY - 1)),
@@ -677,11 +695,11 @@
             jax.ShapeDtypeStruct((D, D), BF16),
             jax.ShapeDtypeStruct((8, 128), F32),
         ),
-        in_specs=[pl.BlockSpec(memory_space=pl.ANY)] * 8,
+        in_specs=[pl.BlockSpec(memory_space=pltpu.HBM)] * 8,
         out_specs=(vmem,) * 4,
         scratch_shapes=ARGUMENT_SCRATCH + LAYER_SCRATCH + SUM_SCRATCH + SEMAPHORES,
         compiler_params=pltpu.CompilerParams(
-            vmem_limit_bytes=52 * 2**20, collective_id=0, has_side_effects=True
+            vmem_limit_bytes=60 * 2**20, collective_id=0, has_side_effects=True
         ),
         name="layer_grads",
     )(tokens, cotangent, weight, out_weight, table, length, first, slot)

time: 68.8 us -> 63.8 us (0.927)
  Pallas kernels: 60.8 us -> 57 us
  local copies, waits for them, and re-layouts: 5.65 us -> 3.73 us
  other arithmetic: 1.1 us -> 2.14 us
    pallas_call x1, Pallas kernels: 60.8 us -> 57 us  [shards(): pl.pallas_call(layer_kernel, out_shape=(jax.ShapeDtypeStruct((ROWS, D), B...]
    unnamed x12 -> x4, local copies, waits for them, and re-layouts: 5.07 us -> 2.47 us
    convert_element_type x1, other arithmetic: 1.1 us -> 2.14 us  [shards(): out_grad.astype(F32)]
where the time goes in v3:
time: 63.8 us; the launch traced here: 63.5 us
  Pallas kernels  57 us (89%)
  local copies, waits for them, and re-layouts  3.73 us (6%)
  other arithmetic  2.14 us (3%)
  between operations  0.65 us (1%)
    pallas_call x1, Pallas kernels, shards(): pl.pallas_call(layer_kernel, out_shape=(jax.ShapeDtypeStruct((ROWS, D), B...  57 us
    unnamed x4, local copies, waits for them, and re-layouts  2.47 us
    convert_element_type x1, other arithmetic, shards(): out_grad.astype(F32)  2.14 us

profile of v3, /device:TPU:1, one launch (start us, length us, event | category | flops | bytes accessed | tf_op | source)
XLA Modules:
  0.0 63.5 jit_solution(15651496377831851998)
XLA Ops:
  0.6 57.0 %layer_grads.1 = (bf16[512,512]{1,0:T(8,128)(2,1)}, f32[4,512]{1,0:T(4,128)}, bf16[512,512]{1,0:T(8,128)(2,1)}, f32[8,128]{1,0:T(8,128)}) custom-call(bf16[512,512]{1,0:T(8,128)(2,1)} %tokens_hbm.1, bf16[768,512]{1,0:T(8,128)(2,1)} %cotangent_hbm.1, bf16[512,2048]{1,0:T(8,128)(2,1)} %weight_hbm.1, bf16[512,512]{1,0:T(8,128)(2,1)} %out_weight_hbm.1, ...), custom_call_target="tpu_custom_call" | custom-call | tf_op jit(solution)/shard_map/layer_grads/pallas_call | solution.py:690
  57.6 0.0 copy-start
  57.7 1.3 %slice.3 = f32[4,10]{1,0:T(4,128)} slice(f32[8,128]{1,0:T(8,128)} %get-tuple-element.11), slice={[0:4], [0:10]} | slice | bytes 320 | tf_op jit(solution)/shard_map/slice | solution.py:706
  58.9 2.1 %convert_element_type.3 = f32[512,512]{1,0:T(8,128)} convert(bf16[512,512]{1,0:T(8,128)(2,1)} %get-tuple-element.10) | non-fusion elementwise | flops 262144 | bytes 1572864 | tf_op jit(solution)/shard_map/convert_element_type | solution.py:706
  61.1 1.9 %copy.14 = bf16[512,512]{1,0:T(8,128)(2,1)} copy(bf16[512,512]{1,0:T(8,128)(2,1)} %get-tuple-element.16) | data formatting | bytes 1048576
  62.9 0.0 copy-done
  62.9 0.6 copy.15
Async XLA Ops:
  57.6 5.3 %copy-start = (f32[4,512]{1,0:T(4,128)S(1)}, f32[4,512]{1,0:T(4,128)}, u32[]{:S(2)}) copy-start(f32[4,512]{1,0:T(4,128)} %get-tuple-element.9) | copy-start | bytes 24580

commit v4 on v3

--- a/solution.py
+++ b/solution.py
@@ -61,14 +61,20 @@
     lax.fori_loop(0, BLOCKS, body, 0)
 
 
+def head_weight(weight_ref, head, groups):
+    parts = [weight_ref[:, pl.ds(pl.multiple_of(g * D + head * 128, 128), 128)] for g in groups]
+    return jnp.concatenate(parts, axis=1)
+
+
 def project(head, normed_b_ref, weight_ref, acts_ref, slope_ref):
-    for c in range(2):
-        lanes = pl.ds(c * 256, 256)
-        half = dot(normed_b_ref[...], weight_ref[head, :, lanes]) * 0.5
-        u = 1.0 + jnp.tanh(half)
-        act = half * u
-        slope_ref[head, :, lanes] = 0.5 * (u + act * (2.0 - u))
-        acts_ref[head, :, lanes] = act.astype(BF16)
+    for r in range(2):
+        for c in range(2):
+            rows, lanes = pl.ds(r * 256, 256), pl.ds(c * 256, 256)
+            half = dot(normed_b_ref[rows, :], head_weight(weight_ref, head, (2 * c, 2 * c + 1))) * 0.5
+            u = 1.0 + jnp.tanh(half)
+            act = half * u
+            slope_ref[head, rows, lanes] = 0.5 * (u + act * (2.0 - u))
+            acts_ref[head, rows, lanes] = act.astype(BF16)
 
 
 def take_upstream(own_ref, received_ref, slot_ref, length_ref, first_ref, upstream_ref):
@@ -100,38 +106,52 @@
     return distance, [(bucket, 0 if bucket == 0 else 2 ** (bucket - 1)) for bucket in BUCKETS_AT[apart]]
 
 
-def bias_tiles(table_ref, head):
-    tiles = []
-    for apart in range(BLOCKS):
-        distance, bounds = bucket_bounds(apart)
-        tile = jnp.full((BLOCK, BLOCK), table_ref[head, bounds[0][0]] * 0.5, F32)
-        for bucket, least in bounds[1:]:
-            tile = jnp.where(distance >= least, table_ref[head, bucket] * 0.5, tile)
-        tiles.append(tile)
-    return tiles
-
-
-def attend(head, acts_ref, table_ref, length_ref, first_ref, weights_ref, factor_ref, attended_ref):
-    bias = bias_tiles(table_ref, head)
+def tile_rows(i):
+    return slice(i * BLOCK, (i + 1) * BLOCK)
+
+
+def fill_bias(table_ref, bias_tile_ref):
+    def body(head, carry):
+        for apart in range(BLOCKS):
+            distance, bounds = bucket_bounds(apart)
+            tile = jnp.full((BLOCK, BLOCK), table_ref[head, bounds[0][0]] * 0.5, F32)
+            for bucket, least in bounds[1:]:
+                tile = jnp.where(distance >= least, table_ref[head, bucket] * 0.5, tile)
+            bias_tile_ref[head, apart] = tile
+        return carry
+
+    lax.fori_loop(0, HEADS, body, 0)
+
+
+def clear_upper(weights_ref, d_logits_ref):
+    zero = jnp.zeros((BLOCK, BLOCK), BF16)
+    for i in (0, 2):
+        d_logits_ref[tile_rows(i), tile_rows(i + 1)] = zero
+        for head in range(HEADS):
+            weights_ref[head, tile_rows(i), tile_rows(i + 1)] = zero
+
+
+def attend(head, acts_ref, bias_tile_ref, length_ref, first_ref, weights_ref, factor_ref, attended_ref):
     row = tile_iota(0)
     causal_row = jnp.where(tile_iota(1) <= row, row, ROWS)
-    for i in range(BLOCKS):
-        rows = pl.ds(i * BLOCK, BLOCK)
-        upto = (i + 1) * BLOCK
-        scores = dot_right_t(acts_ref[head, rows, QUERY], acts_ref[head, 0:upto, KEY])
-        for j in range(i + 1):
-            lanes = pl.ds(j * BLOCK, BLOCK)
-            limit = jnp.where(
-                first_ref[i] == first_ref[j], length_ref[i] - (i - first_ref[i]) * BLOCK, 0
-            )
-            half = scores[:, j * BLOCK : (j + 1) * BLOCK] * (0.5 * SCALE) + bias[i - j]
-            kept = (causal_row if i == j else row) < limit
-            u = jnp.where(kept, 1.0 + jnp.tanh(half), 0.0)
-            weight = half * u
-            factor_ref[head, rows, lanes] = 0.5 * (u + weight * (2.0 - u))
-            weights_ref[head, rows, lanes] = weight.astype(BF16)
-        attended_ref[head, rows, :] = dot(
-            weights_ref[head, rows, 0:upto], acts_ref[head, 0:upto, VALUE]
+    for pair in range(2):
+        upto = (pair + 1) * 256
+        pair_rows = pl.ds(pair * 256, 256)
+        scores = dot_right_t(acts_ref[head, pair_rows, QUERY], acts_ref[head, 0:upto, KEY])
+        for i in (2 * pair, 2 * pair + 1):
+            at = (i - 2 * pair) * BLOCK
+            for j in range(i + 1):
+                limit = jnp.where(
+                    first_ref[i] == first_ref[j], length_ref[i] - (i - first_ref[i]) * BLOCK, 0
+                )
+                half = scores[at : at + BLOCK, tile_rows(j)] * (0.5 * SCALE) + bias_tile_ref[head, i - j]
+                kept = (causal_row if i == j else row) < limit
+                u = jnp.where(kept, 1.0 + jnp.tanh(half), 0.0)
+                weight = half * u
+                factor_ref[head, tile_rows(i), tile_rows(j)] = 0.5 * (u + weight * (2.0 - u))
+                weights_ref[head, tile_rows(i), tile_rows(j)] = weight.astype(BF16)
+        attended_ref[head, pair_rows, :] = dot(
+            weights_ref[head, pair_rows, 0:upto], acts_ref[head, 0:upto, VALUE]
         )
 
 
@@ -159,50 +179,62 @@
 
 
 def attend_back(
-    head, acts_ref, weights_ref, factor_ref, d_attended_ref, slope_ref, d_logits_ref, d_proj_ref, bias_ref
+    head, acts_ref, weights_ref, factor_ref, d_attended_ref, slope_ref, d_logits_ref, d_proj_ref, sums_ref
 ):
     sums = [None] * BLOCKS
-    for i in range(BLOCKS):
-        rows = pl.ds(i * BLOCK, BLOCK)
-        upto = (i + 1) * BLOCK
-        d_weights = dot_right_t(d_attended_ref[head, rows, :], acts_ref[head, 0:upto, VALUE])
-        for j in range(i + 1):
-            lanes = pl.ds(j * BLOCK, BLOCK)
-            d_logits = d_weights[:, j * BLOCK : (j + 1) * BLOCK] * factor_ref[head, rows, lanes]
-            sums[i - j] = d_logits if sums[i - j] is None else sums[i - j] + d_logits
-            d_logits_ref[rows, lanes] = d_logits.astype(BF16)
-        d_query = dot(d_logits_ref[rows, 0:upto], acts_ref[head, 0:upto, KEY])
-        d_proj_ref[head, rows, QUERY] = (d_query * SCALE * slope_ref[head, rows, QUERY]).astype(BF16)
-    for j in range(BLOCKS):
-        rows = pl.ds(j * BLOCK, BLOCK)
-        below = pl.ds(j * BLOCK, ROWS - j * BLOCK)
-        d_value = dot_left_t(weights_ref[head, below, rows], d_attended_ref[head, below, :])
-        d_proj_ref[head, rows, VALUE] = (d_value * slope_ref[head, rows, VALUE]).astype(BF16)
-        d_key = dot_left_t(d_logits_ref[below, rows], acts_ref[head, below, QUERY])
-        d_proj_ref[head, rows, KEY] = (d_key * SCALE * slope_ref[head, rows, KEY]).astype(BF16)
-    totals = [None] * BUCKETS
+    for pair in range(2):
+        upto = (pair + 1) * 256
+        pair_rows = pl.ds(pair * 256, 256)
+        d_weights = dot_right_t(d_attended_ref[head, pair_rows, :], acts_ref[head, 0:upto, VALUE])
+        for i in (2 * pair, 2 * pair + 1):
+            at = (i - 2 * pair) * BLOCK
+            for j in range(i + 1):
+                d_logits = d_weights[at : at + BLOCK, tile_rows(j)] * factor_ref[head, tile_rows(i), tile_rows(j)]
+                sums[i - j] = d_logits if sums[i - j] is None else sums[i - j] + d_logits
+                d_logits_ref[tile_rows(i), tile_rows(j)] = d_logits.astype(BF16)
+        d_query = dot(d_logits_ref[pair_rows, 0:upto], acts_ref[head, 0:upto, KEY])
+        d_proj_ref[head, pair_rows, QUERY] = (d_query * SCALE * slope_ref[head, pair_rows, QUERY]).astype(BF16)
     for apart in range(BLOCKS):
-        distance, bounds = bucket_bounds(apart)
-        for at, (bucket, least) in enumerate(bounds):
-            value = sums[apart]
-            if at > 0:
-                value = jnp.where(distance >= least, value, 0.0)
-            if at + 1 < len(bounds):
-                value = jnp.where(distance < bounds[at + 1][1], value, 0.0)
-            value = jnp.sum(value, axis=0, keepdims=True)
-            totals[bucket] = value if totals[bucket] is None else totals[bucket] + value
+        sums_ref[head, apart] = sums[apart]
+    for pair in range(2):
+        pair_rows = pl.ds(pair * 256, 256)
+        below = pl.ds(pair * 256, ROWS - pair * 256)
+        d_value = dot_left_t(weights_ref[head, below, pair_rows], d_attended_ref[head, below, :])
+        d_proj_ref[head, pair_rows, VALUE] = (d_value * slope_ref[head, pair_rows, VALUE]).astype(BF16)
+        d_key = dot_left_t(d_logits_ref[below, pair_rows], acts_ref[head, below, QUERY])
+        d_proj_ref[head, pair_rows, KEY] = (d_key * SCALE * slope_ref[head, pair_rows, KEY]).astype(BF16)
+
+
+def bias_sums(sums_ref, bias_ref):
     lane = lax.broadcasted_iota(jnp.int32, (1, 128), 1)
-    packed = jnp.zeros((1, 128), F32)
-    for bucket in range(BUCKETS):
-        packed = jnp.where(lane == bucket, jnp.sum(totals[bucket], axis=1, keepdims=True), packed)
-    bias_ref[pl.ds(head, 1), :] = packed
+    bias_ref[...] = jnp.zeros_like(bias_ref)
+
+    def body(head, carry):
+        totals = [None] * BUCKETS
+        for apart in range(BLOCKS):
+            distance, bounds = bucket_bounds(apart)
+            for at, (bucket, least) in enumerate(bounds):
+                value = sums_ref[head, apart]
+                if at > 0:
+                    value = jnp.where(distance >= least, value, 0.0)
+                if at + 1 < len(bounds):
+                    value = jnp.where(distance < bounds[at + 1][1], value, 0.0)
+                value = jnp.sum(value, axis=0, keepdims=True)
+                totals[bucket] = value if totals[bucket] is None else totals[bucket] + value
+        packed = jnp.zeros((1, 128), F32)
+        for bucket in range(BUCKETS):
+            packed = jnp.where(lane == bucket, jnp.sum(totals[bucket], axis=1, keepdims=True), packed)
+        bias_ref[pl.ds(head, 1), :] = packed
+        return carry
+
+    lax.fori_loop(0, HEADS, body, 0)
 
 
 def token_grads(part, d_proj_ref, weight_ref, normed_ref, inverse_ref, upstream_ref, token_grad_ref):
     rows = pl.ds(part * 256, 256)
-    d_normed = dot_right_t(d_proj_ref[0, rows, :], weight_ref[0])
+    d_normed = dot_right_t(d_proj_ref[0, rows, :], head_weight(weight_ref, 0, range(4)))
     for h in range(1, HEADS):
-        d_normed = d_normed + dot_right_t(d_proj_ref[h, rows, :], weight_ref[h])
+        d_normed = d_normed + dot_right_t(d_proj_ref[h, rows, :], head_weight(weight_ref, h, range(4)))
     normed = normed_ref[rows, :]
     inverse = inverse_ref[rows, 0:1]
     mean = jnp.mean(d_normed, axis=-1, keepdims=True)
@@ -225,7 +257,7 @@
     token_grad_ref, proj_grad_ref, out_grad_ref, bias_grad_ref,
     tokens_ref, own_ref, received_ref, weight_ref, out_weight_ref, table_ref, length_ref, first_ref, slot_ref,
     normed_ref, normed_b_ref, inverse_ref, acts_ref, slope_ref, upstream_ref, d_mixed_ref, weights_ref,
-    factor_ref, attended_ref, mixed_ref, d_attended_ref, d_logits_ref, d_proj_ref,
+    factor_ref, attended_ref, mixed_ref, d_attended_ref, d_logits_ref, d_proj_ref, bias_tile_ref, sums_ref,
     term, core_in, x_out, x_in, x_sum, y_in, y_sum, z_in,
     out_y_in, out_z_all, out_mine, out_x_all, out_core_in,
     bias_core, bias_x, bias_y, bias_z,
@@ -262,16 +294,8 @@
         pltpu.make_async_copy(cotangent_hbm.at[pl.ds(0, ROWS)], own_ref, load_sem.at[5]),
         pltpu.make_async_copy(out_weight_hbm, out_weight_ref, load_sem.at[6]),
     ]
-
-    def weight_load(h, g):
-        return pltpu.make_async_copy(
-            weight_hbm.at[:, pl.ds(pl.multiple_of(g * D + h * 128, 128), 128)],
-            weight_ref.at[h, :, pl.ds(g * 128, 128)],
-            load_sem.at[7 + h * 4 + g],
-        )
-
-    weight_loads = [weight_load(h, g) for h in range(HEADS) for g in range(4)]
-    for load in loads[:1] + weight_loads + loads[1:]:
+    weight_load = pltpu.make_async_copy(weight_hbm, weight_ref, load_sem.at[7])
+    for load in loads[:2] + [weight_load] + loads[2:]:
         load.start()
 
     barrier = pltpu.get_barrier_semaphore()
@@ -283,6 +307,9 @@
     for target in greeted:
         pl.semaphore_signal(barrier, inc=1, device_id=target, device_id_type=pl.DeviceIdType.MESH)
 
+    clear_upper(weights_ref, d_logits_ref)
+    loads[1].wait()
+    fill_bias(table_ref, bias_tile_ref)
     loads[0].wait()
     norm_tokens(tokens_ref, normed_ref, normed_b_ref, inverse_ref)
 
@@ -293,14 +320,14 @@
     )
     cotangent_copy.start()
 
-    for load in loads[1:5]:
+    for load in loads[2:5]:
         load.wait()
 
+    weight_load.wait()
+
     def forward(head, carry):
-        for g in range(4):
-            weight_load(head, g).wait()
         project(head, normed_b_ref, weight_ref, acts_ref, slope_ref)
-        attend(head, acts_ref, table_ref, length_ref, first_ref, weights_ref, factor_ref, attended_ref)
+        attend(head, acts_ref, bias_tile_ref, length_ref, first_ref, weights_ref, factor_ref, attended_ref)
         return carry
 
     lax.fori_loop(0, HEADS, forward, 0)
@@ -429,11 +456,16 @@
             out_y_back_sem.at[1, k - 1], device(x, y_peer(k), z, core),
         )
 
-    def out_x_back_copy(k):
+    def out_x_back_copy(k, steps):
         return remote(
-            out_mine, out_x_all.at[x], out_x_back_sem.at[0, k - 1], out_x_back_sem.at[1, k - 1],
+            out_chunk(out_mine, y_peer(steps)), out_chunk(out_x_all, y_peer(steps), x),
+            out_x_back_sem.at[0, k - 1, steps], out_x_back_sem.at[1, k - 1, steps],
             device(x_peer(k), y, z, core),
         )
+
+    def out_x_back_start(steps):
+        for k in (2, 1, 3):
+            out_x_back_copy(k, steps).start()
 
     out_core_back_copy = remote(
         out_x_all, out_core_in, out_core_back_sem.at[0], out_core_back_sem.at[1], device(x, y, z, other)
@@ -460,19 +492,20 @@
         for k in range(1, NZ):
             total = total + out_z_all[k].astype(F32)
         out_chunk(out_mine, y)[...] = total.astype(BF16)
-        for k in range(1, NY):
+        for k in (4, 3, 5, 2, 6, 1, 7):
             out_y_back_copy(k).start()
+        out_x_back_start(0)
 
     def out_after_y_back():
-        for k in range(1, NY):
+        for k in (1, 7, 2, 6, 3, 5, 4):
             out_y_back_copy(k).wait_recv()
+            out_x_back_start(NY - k)
         out_x_all[x] = out_mine[...]
-        for k in range(1, NX):
-            out_x_back_copy(k).start()
 
     def out_after_x_back():
         for k in range(1, NX):
-            out_x_back_copy(k).wait_recv()
+            for steps in range(NY):
+                out_x_back_copy(k, steps).wait_recv()
         out_core_back_copy.start()
 
     def out_finish():
@@ -520,7 +553,7 @@
     def back(head):
         attend_back(
             head, acts_ref, weights_ref, factor_ref, d_attended_ref, slope_ref, d_logits_ref, d_proj_ref,
-            bias_grad_ref,
+            sums_ref,
         )
 
     def send_head(head):
@@ -542,7 +575,6 @@
     d_gate = jnp.concatenate([d_proj_ref[h, :, GATE] for h in range(HEADS)], axis=1)
     put_term(1, dot_left_t(d_gate, normed_b_ref[...]))
     core_copy(1).start()
-    bias_grad_ref[...] = jnp.zeros_like(bias_grad_ref)
     after_core(0)
     back(0)
     after_core(1)
@@ -560,40 +592,33 @@
     after_x(1)
     y_start(gate_units)
     send_head(3)
+    out_after_y()
+    bias_sums(sums_ref, bias_grad_ref)
     bias_start(0, bias_grad_ref[...])
+    after_core(5)
     tokens_part(0)
-    after_core(5)
     bias_start(1, bias_finish(0))
-    tokens_part(1)
     after_x(2)
     y_start(head_units(0))
-    out_after_y()
     after_x(3)
     y_start(head_units(1))
+    tokens_part(1)
+    out_after_z()
     after_x(4)
     y_start(head_units(2))
-    bias_start(2, bias_finish(1))
     after_x(5)
     y_start(head_units(3))
-    out_after_z()
+    bias_start(2, bias_finish(1))
     after_y_gate()
-    for h in range(HEADS - 1):
-        after_y(h)
+    after_y(0)
+    after_y(1)
+    out_after_y_back()
     bias_start(3, bias_finish(2))
-    out_after_y_back()
-    after_y(HEADS - 1)
-    for k in range(1, NZ):
+    after_y(2)
+    after_y(3)
+    for k in (4, 3, 5, 2, 6, 1, 7):
         z_copy(k).start()
     out_after_x_back()
-    for k in range(1, NZ):
-        z_copy(k).wait_recv()
-    total = y_sum[lax.div(z, 4), lax.rem(z, 4)].astype(F32)
-    for k in range(NZ - 1):
-        total = total + z_in[k].astype(F32)
-    for q in range(4):
-        proj_grad_ref[:, q * 128 : (q + 1) * 128] = total[4 * q : 4 * q + 4]
-    bias_grad_ref[...] = bias_finish(3)
-    out_finish()
 
     cotangent_copy.wait_send()
     for s in range(SETS):
@@ -609,13 +634,25 @@
         out_y_back_copy(k).wait_send()
     for k in range(1, NZ):
         out_z_copy(k).wait_send()
-        z_copy(k).wait_send()
     for k in range(1, NX):
-        out_x_back_copy(k).wait_send()
-    out_core_back_copy.wait_send()
+        for steps in range(NY):
+            out_x_back_copy(k, steps).wait_send()
     for step in range(4):
         for copy in bias_copies(step):
             copy.wait_send()
+
+    out_finish()
+    bias_grad_ref[...] = bias_finish(3)
+    for k in range(1, NZ):
+        z_copy(k).wait_recv()
+    total = y_sum[lax.div(z, 4), lax.rem(z, 4)].astype(F32)
+    for k in range(NZ - 1):
+        total = total + z_in[k].astype(F32)
+    for q in range(4):
+        proj_grad_ref[:, q * 128 : (q + 1) * 128] = total[4 * q : 4 * q + 4]
+    for k in range(1, NZ):
+        z_copy(k).wait_send()
+    out_core_back_copy.wait_send()
 
 
 DMA = pltpu.SemaphoreType.DMA
@@ -623,7 +660,7 @@
     pltpu.VMEM((ROWS, D), BF16),
     pltpu.VMEM((ROWS, D), BF16),
     pltpu.VMEM((2 * BLOCK, D), BF16),
-    pltpu.VMEM((HEADS, D, D), BF16),
+    pltpu.VMEM((D, 4 * D), BF16),
     pltpu.VMEM((D, D), BF16),
     pltpu.SMEM((HEADS, BUCKETS), F32),
     pltpu.SMEM((BLOCKS,), jnp.int32),
@@ -645,6 +682,8 @@
     pltpu.VMEM((HEADS, ROWS, 128), BF16),
     pltpu.VMEM((ROWS, ROWS), BF16),
     pltpu.VMEM((HEADS, ROWS, D), BF16),
+    pltpu.VMEM((HEADS, BLOCKS, BLOCK, BLOCK), F32),
+    pltpu.VMEM((HEADS, BLOCKS, BLOCK, BLOCK), F32),
 ]
 SUM_SCRATCH = [
     pltpu.VMEM((SETS, 4, 4, 2, 16, D), BF16),
@@ -666,7 +705,7 @@
     pltpu.VMEM((NZ, 8, 128), F32),
 ]
 SEMAPHORES = [
-    DMA((23,)),
+    DMA((8,)),
     DMA((2,)),
     DMA((2, SETS)),
     DMA((2, SETS, NX - 1)),
@@ -676,13 +715,47 @@
     DMA((2, NY - 1)),
     DMA((2, NZ - 1)),
     DMA((2, NY - 1)),
-    DMA((2, NX - 1)),
+    DMA((2, NX - 1, NY)),
     DMA((2,)),
     DMA((2, 1)),
     DMA((2, NX - 1)),
     DMA((2, NY - 1)),
     DMA((2, NZ - 1)),
 ]
+
+
+def finish_kernel(token_ref, proj_ref, out_ref, bias_ref, token_hbm, proj_hbm, out_hbm, small_ref, wide_ref, sems):
+    copies = [
+        pltpu.make_async_copy(token_ref, token_hbm, sems.at[0]),
+        pltpu.make_async_copy(proj_ref, proj_hbm, sems.at[1]),
+        pltpu.make_async_copy(wide_ref, out_hbm, sems.at[2]),
+    ]
+    copies[0].start()
+    copies[1].start()
+    wide_ref[...] = out_ref[...].astype(F32)
+    copies[2].start()
+    small_ref[...] = bias_ref[0:HEADS, 0:BUCKETS]
+    for copy in copies:
+        copy.wait()
+
+
+def finish(*values):
+    vmem = pl.BlockSpec(memory_space=pltpu.VMEM)
+    hbm = pl.BlockSpec(memory_space=pltpu.HBM)
+    return pl.pallas_call(
+        finish_kernel,
+        out_shape=(
+            jax.ShapeDtypeStruct((ROWS, D), BF16),
+            jax.ShapeDtypeStruct((4, D), F32),
+            jax.ShapeDtypeStruct((D, D), F32),
+            jax.ShapeDtypeStruct((HEADS, BUCKETS), F32),
+        ),
+        in_specs=[vmem] * 4,
+        out_specs=(hbm, hbm, hbm, vmem),
+        scratch_shapes=[pltpu.VMEM((D, D), F32), DMA((3,))],
+        compiler_params=pltpu.CompilerParams(vmem_limit_bytes=8 * 2**20),
+        name="finish",
+    )(*values)
 
 
 def shards(tokens, cotangent, weight, out_weight, table, length, first, slot):
@@ -699,11 +772,15 @@
         out_specs=(vmem,) * 4,
         scratch_shapes=ARGUMENT_SCRATCH + LAYER_SCRATCH + SUM_SCRATCH + SEMAPHORES,
         compiler_params=pltpu.CompilerParams(
-            vmem_limit_bytes=60 * 2**20, collective_id=0, has_side_effects=True
+            vmem_limit_bytes=52 * 2**20, collective_id=0, has_side_effects=True
         ),
         name="layer_grads",
-    )(tokens, cotangent, weight, out_weight, table, length, first, slot)
-    return token_grad, proj_grad.T, out_grad.astype(F32), bias_grad[:HEADS, :BUCKETS]
+    )(*(
+        pltpu.with_memory_space_constraint(value, pltpu.HBM)
+        for value in (tokens, cotangent, weight, out_weight, table, length, first, slot)
+    ))
+    token_grad, proj_grad, out_grad, bias_grad = finish(token_grad, proj_grad, out_grad, bias_grad)
+    return token_grad, proj_grad.T, out_grad, bias_grad
 
 
 def solution(mesh):

time: 63.8 us -> 55.5 us (0.87)
  local copies, waits for them, and re-layouts: 3.73 us -> 0 us
  Pallas kernels: 57 us -> 54.5 us
  other arithmetic: 2.14 us -> 0 us
    pallas_call x1, Pallas kernels: 57 us -> 52.7 us  [shards(): pl.pallas_call(layer_kernel, out_shape=(jax.ShapeDtypeStruct((ROWS, D), B...]
    unnamed x4 -> x0, local copies, waits for them, and re-layouts: 2.47 us -> none
    convert_element_type x1 -> x0, other arithmetic: 2.14 us -> none  [shards(): out_grad.astype(F32)]
    pallas_call x0 -> x1, Pallas kernels: none -> 1.75 us  [finish(): pl.pallas_call(finish_kernel, out_shape=(jax.ShapeDtypeStruct((ROWS, D),...]
    slice x1 -> x0, local copies, waits for them, and re-layouts: 1.26 us -> none  [shards(): bias_grad[:HEADS, :BUCKETS]]
where the time goes in v4:
time: 55.5 us; the launch traced here: 55.1 us
  Pallas kernels  54.5 us (98%)
  between operations  0.64 us (1%)
    pallas_call x1, Pallas kernels, shards(): pl.pallas_call(layer_kernel, out_shape=(jax.ShapeDtypeStruct((ROWS, D), B...  52.7 us
    pallas_call x1, Pallas kernels, finish(): pl.pallas_call(finish_kernel, out_shape=(jax.ShapeDtypeStruct((ROWS, D),...  1.75 us

profile of v4, /device:TPU:1, one launch (start us, length us, event | category | flops | bytes accessed | tf_op | source)
XLA Modules:
  0.0 55.1 jit_solution(4032593366665912443)
XLA Ops:
  0.6 52.7 %layer_grads.1 = (bf16[512,512]{1,0:T(8,128)(2,1)S(1)}, f32[4,512]{1,0:T(4,128)S(1)}, bf16[512,512]{1,0:T(8,128)(2,1)S(1)}, f32[8,128]{1,0:T(8,128)S(1)}) custom-call(bf16[512,512]{1,0:T(8,128)(2,1)} %tokens_hbm.1, bf16[768,512]{1,0:T(8,128)(2,1)} %cotangent_hbm.1, bf16[512,2048]{1,0:T(8,128)(2,1)} %weight_hbm.1, bf16[512,512]{1,0:T(8,128)(2,1)} %out_weight_hbm.1, ...), custom_call_target="tpu_custom_call" | custom-call | tf_op jit(solution)/shard_map/layer_grads/pallas_call | solution.py:763
  53.4 1.8 %finish.1 = (bf16[512,512]{1,0:T(8,128)(2,1)}, f32[4,512]{1,0:T(4,128)}, f32[512,512]{1,0:T(8,128)}, f32[4,10]{1,0:T(4,128)}) custom-call(bf16[512,512]{1,0:T(8,128)(2,1)S(1)} %get-tuple-element.12.token_ref, f32[4,512]{1,0:T(4,128)S(1)} %get-tuple-element.13.proj_ref, bf16[512,512]{1,0:T(8,128)(2,1)S(1)} %get-tuple-element.14.out_ref, ...), custom_call_target="tpu_custom_call" | custom-call | tf_op jit(solution)/shard_map/finish/pallas_call | solution.py:745

commit v5 on v4

--- a/solution.py
+++ b/solution.py
@@ -47,8 +47,8 @@
 
 
 def norm_tokens(tokens_ref, normed_ref, normed_b_ref, inverse_ref):
-    def body(b, carry):
-        rows = pl.ds(pl.multiple_of(b * BLOCK, BLOCK), BLOCK)
+    for b in range(BLOCKS):
+        rows = pl.ds(b * BLOCK, BLOCK)
         x = tokens_ref[rows, :].astype(F32)
         centered = x - jnp.mean(x, axis=-1, keepdims=True)
         inverse = lax.rsqrt(jnp.mean(centered * centered, axis=-1, keepdims=True) + EPSILON)
@@ -56,13 +56,10 @@
         normed_ref[rows, :] = normed
         normed_b_ref[rows, :] = normed.astype(BF16)
         inverse_ref[rows, :] = jnp.broadcast_to(inverse, (BLOCK, BLOCK))
-        return carry
-
-    lax.fori_loop(0, BLOCKS, body, 0)
 
 
 def head_weight(weight_ref, head, groups):
-    parts = [weight_ref[:, pl.ds(pl.multiple_of(g * D + head * 128, 128), 128)] for g in groups]
+    parts = [weight_ref[:, pl.ds(g * D + head * 128, 128)] for g in groups]
     return jnp.concatenate(parts, axis=1)
 
 
@@ -78,8 +75,8 @@
 
 
 def take_upstream(own_ref, received_ref, slot_ref, length_ref, first_ref, upstream_ref):
-    def body(b, carry):
-        rows = pl.ds(pl.multiple_of(b * BLOCK, BLOCK), BLOCK)
+    for b in range(BLOCKS):
+        rows = pl.ds(b * BLOCK, BLOCK)
         slot = jnp.full((BLOCK, D), lax.rem(slot_ref[b], SLOTS), jnp.int32)
         value = own_ref[0:BLOCK, :].astype(F32)
         for at in range(1, SLOTS):
@@ -89,9 +86,6 @@
         row = lax.broadcasted_iota(jnp.int32, (BLOCK, D), 0)
         value = jnp.where(row < limit, value, 0.0)
         upstream_ref[rows, :] = value.astype(BF16)
-        return carry
-
-    lax.fori_loop(0, BLOCKS, body, 0)
 
 
 def mix_back(upstream_ref, out_weight_ref, d_mixed_ref):
@@ -156,8 +150,8 @@
 
 
 def mix(acts_ref, attended_ref, d_mixed_ref, slope_ref, mixed_ref, d_attended_ref, d_proj_ref):
-    def body(b, carry):
-        rows = pl.ds(pl.multiple_of(b * BLOCK, BLOCK), BLOCK)
+    for b in range(BLOCKS):
+        rows = pl.ds(b * BLOCK, BLOCK)
         heads = range(HEADS)
         att = [attended_ref[h, rows, :] for h in heads]
         mean = row_sum(att) * (1.0 / D)
@@ -173,9 +167,6 @@
             mixed_ref[rows, pl.ds(h * 128, 128)] = (normed[h] * gate[h]).astype(BF16)
             d_attended_ref[h, rows, :] = (inverse * (g[h] - g_mean - normed[h] * g_dot)).astype(BF16)
             d_proj_ref[h, rows, GATE] = (d_mixed[h] * normed[h] * slope_ref[h, rows, GATE]).astype(BF16)
-        return carry
-
-    lax.fori_loop(0, BLOCKS, body, 0)
 
 
 def attend_back(
@@ -209,7 +200,7 @@
     lane = lax.broadcasted_iota(jnp.int32, (1, 128), 1)
     bias_ref[...] = jnp.zeros_like(bias_ref)
 
-    def body(head, carry):
+    for head in range(HEADS):
         totals = [None] * BUCKETS
         for apart in range(BLOCKS):
             distance, bounds = bucket_bounds(apart)
@@ -225,9 +216,6 @@
         for bucket in range(BUCKETS):
             packed = jnp.where(lane == bucket, jnp.sum(totals[bucket], axis=1, keepdims=True), packed)
         bias_ref[pl.ds(head, 1), :] = packed
-        return carry
-
-    lax.fori_loop(0, HEADS, body, 0)
 
 
 def token_grads(part, d_proj_ref, weight_ref, normed_ref, inverse_ref, upstream_ref, token_grad_ref):
@@ -325,12 +313,11 @@
 
     weight_load.wait()
 
-    def forward(head, carry):
-        project(head, normed_b_ref, weight_ref, acts_ref, slope_ref)
+    project(0, normed_b_ref, weight_ref, acts_ref, slope_ref)
+    for head in range(HEADS):
+        if head + 1 < HEADS:
+            project(head + 1, normed_b_ref, weight_ref, acts_ref, slope_ref)
         attend(head, acts_ref, bias_tile_ref, length_ref, first_ref, weights_ref, factor_ref, attended_ref)
-        return carry
-
-    lax.fori_loop(0, HEADS, forward, 0)
 
     for load in loads[5:]:
         load.wait()

time: 55.5 us -> 54 us (0.973)
  Pallas kernels: 54.5 us -> 53.2 us
    pallas_call x1, Pallas kernels: 52.7 us -> 51.4 us  [shards(): pl.pallas_call(layer_kernel, out_shape=(jax.ShapeDtypeStruct((ROWS, D), B...]
where the time goes in v5:
time: 54 us; the launch traced here: 53.8 us
  Pallas kernels  53.2 us (99%)
  between operations  0.64 us (1%)
    pallas_call x1, Pallas kernels, shards(): pl.pallas_call(layer_kernel, out_shape=(jax.ShapeDtypeStruct((ROWS, D), B...  51.4 us
    pallas_call x1, Pallas kernels, finish(): pl.pallas_call(finish_kernel, out_shape=(jax.ShapeDtypeStruct((ROWS, D),...  1.75 us

profile of v5, /device:TPU:1, one launch (start us, length us, event | category | flops | bytes accessed | tf_op | source)
XLA Modules:
  0.0 53.8 jit_solution(5034983747266861588)
XLA Ops:
  0.6 51.4 %layer_grads.1 = (bf16[512,512]{1,0:T(8,128)(2,1)S(1)}, f32[4,512]{1,0:T(4,128)S(1)}, bf16[512,512]{1,0:T(8,128)(2,1)S(1)}, f32[8,128]{1,0:T(8,128)S(1)}) custom-call(bf16[512,512]{1,0:T(8,128)(2,1)} %tokens_hbm.1, bf16[768,512]{1,0:T(8,128)(2,1)} %cotangent_hbm.1, bf16[512,2048]{1,0:T(8,128)(2,1)} %weight_hbm.1, bf16[512,512]{1,0:T(8,128)(2,1)} %out_weight_hbm.1, ...), custom_call_target="tpu_custom_call" | custom-call | tf_op jit(solution)/shard_map/layer_grads/pallas_call | solution.py:750
  52.1 1.8 %finish.1 = (bf16[512,512]{1,0:T(8,128)(2,1)}, f32[4,512]{1,0:T(4,128)}, f32[512,512]{1,0:T(8,128)}, f32[4,10]{1,0:T(4,128)}) custom-call(bf16[512,512]{1,0:T(8,128)(2,1)S(1)} %get-tuple-element.12.token_ref, f32[4,512]{1,0:T(4,128)S(1)} %get-tuple-element.13.proj_ref, bf16[512,512]{1,0:T(8,128)(2,1)S(1)} %get-tuple-element.14.out_ref, ...), custom_call_target="tpu_custom_call" | custom-call | tf_op jit(solution)/shard_map/finish/pallas_call | solution.py:732

commit v6 on v5

--- a/solution.py
+++ b/solution.py
@@ -149,22 +149,32 @@
         )
 
 
-def mix(acts_ref, attended_ref, d_mixed_ref, slope_ref, mixed_ref, d_attended_ref, d_proj_ref):
+def mix(acts_ref, attended_ref, att_inverse_ref, mixed_ref):
+    heads = range(HEADS)
     for b in range(BLOCKS):
         rows = pl.ds(b * BLOCK, BLOCK)
-        heads = range(HEADS)
         att = [attended_ref[h, rows, :] for h in heads]
         mean = row_sum(att) * (1.0 / D)
         centered = [a - mean for a in att]
         inverse = lax.rsqrt(row_sum([c * c for c in centered]) * (1.0 / D) + EPSILON)
-        normed = [c * inverse for c in centered]
-        gate = [acts_ref[h, rows, GATE].astype(F32) for h in heads]
+        att_inverse_ref[rows, :] = jnp.broadcast_to(inverse, (BLOCK, BLOCK))
+        for h in heads:
+            normed = centered[h] * inverse
+            attended_ref[h, rows, :] = normed
+            mixed_ref[rows, pl.ds(h * 128, 128)] = (normed * acts_ref[h, rows, GATE].astype(F32)).astype(BF16)
+
+
+def mix_grads(acts_ref, attended_ref, att_inverse_ref, d_mixed_ref, slope_ref, d_attended_ref, d_proj_ref):
+    heads = range(HEADS)
+    for b in range(BLOCKS):
+        rows = pl.ds(b * BLOCK, BLOCK)
+        normed = [attended_ref[h, rows, :] for h in heads]
+        inverse = att_inverse_ref[rows, 0:1]
         d_mixed = [d_mixed_ref[h, rows, :] for h in heads]
-        g = [d_mixed[h] * gate[h] for h in heads]
+        g = [d_mixed[h] * acts_ref[h, rows, GATE].astype(F32) for h in heads]
         g_mean = row_sum(g) * (1.0 / D)
         g_dot = row_sum([g[h] * normed[h] for h in heads]) * (1.0 / D)
         for h in heads:
-            mixed_ref[rows, pl.ds(h * 128, 128)] = (normed[h] * gate[h]).astype(BF16)
             d_attended_ref[h, rows, :] = (inverse * (g[h] - g_mean - normed[h] * g_dot)).astype(BF16)
             d_proj_ref[h, rows, GATE] = (d_mixed[h] * normed[h] * slope_ref[h, rows, GATE]).astype(BF16)
 
@@ -245,7 +255,7 @@
     token_grad_ref, proj_grad_ref, out_grad_ref, bias_grad_ref,
     tokens_ref, own_ref, received_ref, weight_ref, out_weight_ref, table_ref, length_ref, first_ref, slot_ref,
     normed_ref, normed_b_ref, inverse_ref, acts_ref, slope_ref, upstream_ref, d_mixed_ref, weights_ref,
-    factor_ref, attended_ref, mixed_ref, d_attended_ref, d_logits_ref, d_proj_ref, bias_tile_ref, sums_ref,
+    factor_ref, attended_ref, mixed_ref, d_attended_ref, d_logits_ref, d_proj_ref, bias_tile_ref, sums_ref, att_inverse_ref,
     term, core_in, x_out, x_in, x_sum, y_in, y_sum, z_in,
     out_y_in, out_z_all, out_mine, out_x_all, out_core_in,
     bias_core, bias_x, bias_y, bias_z,
@@ -323,8 +333,7 @@
         load.wait()
     cotangent_copy.wait_recv()
     take_upstream(own_ref, received_ref, slot_ref, length_ref, first_ref, upstream_ref)
-    mix_back(upstream_ref, out_weight_ref, d_mixed_ref)
-    mix(acts_ref, attended_ref, d_mixed_ref, slope_ref, mixed_ref, d_attended_ref, d_proj_ref)
+    mix(acts_ref, attended_ref, att_inverse_ref, mixed_ref)
 
     def put_term(s, value):
         units = value.shape[0] // 128
@@ -559,6 +568,8 @@
 
     put_term(0, dot_left_t(mixed_ref[...], upstream_ref[...]))
     core_copy(0).start()
+    mix_back(upstream_ref, out_weight_ref, d_mixed_ref)
+    mix_grads(acts_ref, attended_ref, att_inverse_ref, d_mixed_ref, slope_ref, d_attended_ref, d_proj_ref)
     d_gate = jnp.concatenate([d_proj_ref[h, :, GATE] for h in range(HEADS)], axis=1)
     put_term(1, dot_left_t(d_gate, normed_b_ref[...]))
     core_copy(1).start()
@@ -671,6 +682,7 @@
     pltpu.VMEM((HEADS, ROWS, D), BF16),
     pltpu.VMEM((HEADS, BLOCKS, BLOCK, BLOCK), F32),
     pltpu.VMEM((HEADS, BLOCKS, BLOCK, BLOCK), F32),
+    pltpu.VMEM((ROWS, BLOCK), F32),
 ]
 SUM_SCRATCH = [
     pltpu.VMEM((SETS, 4, 4, 2, 16, D), BF16),

time: 54 us -> 54 us (level)
  no operation moved by 1% of the time
where the time goes in v6:
time: 54 us; the launch traced here: 53.7 us
  Pallas kernels  53.1 us (98%)
  between operations  0.64 us (1%)
    pallas_call x1, Pallas kernels, shards(): pl.pallas_call(layer_kernel, out_shape=(jax.ShapeDtypeStruct((ROWS, D), B...  51.3 us
    pallas_call x1, Pallas kernels, finish(): pl.pallas_call(finish_kernel, out_shape=(jax.ShapeDtypeStruct((ROWS, D),...  1.75 us

profile of v6, /device:TPU:1, one launch (start us, length us, event | category | flops | bytes accessed | tf_op | source)
XLA Modules:
  0.0 53.7 jit_solution(15577102002200209120)
XLA Ops:
  0.6 51.3 %layer_grads.1 = (bf16[512,512]{1,0:T(8,128)(2,1)S(1)}, f32[4,512]{1,0:T(4,128)S(1)}, bf16[512,512]{1,0:T(8,128)(2,1)S(1)}, f32[8,128]{1,0:T(8,128)S(1)}) custom-call(bf16[512,512]{1,0:T(8,128)(2,1)} %tokens_hbm.1, bf16[768,512]{1,0:T(8,128)(2,1)} %cotangent_hbm.1, bf16[512,2048]{1,0:T(8,128)(2,1)} %weight_hbm.1, bf16[512,512]{1,0:T(8,128)(2,1)} %out_weight_hbm.1, ...), custom_call_target="tpu_custom_call" | custom-call | tf_op jit(solution)/shard_map/layer_grads/pallas_call | solution.py:762
  52.0 1.8 %finish.1 = (bf16[512,512]{1,0:T(8,128)(2,1)}, f32[4,512]{1,0:T(4,128)}, f32[512,512]{1,0:T(8,128)}, f32[4,10]{1,0:T(4,128)}) custom-call(bf16[512,512]{1,0:T(8,128)(2,1)S(1)} %get-tuple-element.12.token_ref, f32[4,512]{1,0:T(4,128)S(1)} %get-tuple-element.13.proj_ref, bf16[512,512]{1,0:T(8,128)(2,1)S(1)} %get-tuple-element.14.out_ref, ...), custom_call_target="tpu_custom_call" | custom-call | tf_op jit(solution)/shard_map/finish/pallas_call | solution.py:744
